TPU v7x, 256 devices: a whole 4x4x8 slice. The times are simulated.
256 devices in a mesh: row: 32 (over y, z_lo, x), col: 8 (over z_hi, core).
Axes of the slice: x: 4, y: 4, z: 8 (z_hi: 4, z_lo: 2; z = z_hi * 2 + z_lo), core: 2. Of those that a mesh axis runs over, the one named last changes fastest.
Arguments:
- velocity: float32 [3, 32, 256, 4096], P(None, 'col', 'row'), may hold values from -14.4 to 14.4
Outputs:
- leonard: float32 [6, 32, 256, 4096], P(None, 'col', 'row')
- model: float32 [6, 32, 256, 4096], P(None, 'col', 'row')
- stress: float32 [6, 32, 256, 4096], P(None, 'col', 'row')
All inputs are finite; a program needn't handle non-finite values.
Results may differ from a plain program's by a relative error of at most 0.00011.
Values sent between devices are 32-bit elements; how exact they have to be, the bound alone decides.
A program may use at most 320 MiB of HBM per device.

v0:
```python
import jax
import jax.numpy as jnp
from jax import lax
from jax.sharding import PartitionSpec as P

pair_list = ((0, 0), (0, 1), (0, 2), (1, 1), (1, 2), (2, 2))
pair_weight = (1.0, 2.0, 2.0, 1.0, 2.0, 1.0)
filter_taps = (
    1.0 / 25,
    2.0 / 25,
    3.0 / 25,
    4.0 / 25,
    5.0 / 25,
    4.0 / 25,
    3.0 / 25,
    2.0 / 25,
    1.0 / 25,
)


def padded_2(block, sides, width):
    for axis, dim in sides:
        count = lax.axis_size(axis)
        forward = [(i, i + 1) for i in range(count - 1)]
        backward = [(target, source) for source, target in forward]
        low = lax.ppermute(
            lax.slice_in_dim(block, block.shape[dim] - width, None, axis=dim), axis, forward
        )
        high = lax.ppermute(lax.slice_in_dim(block, 0, width, axis=dim), axis, backward)
        block = jnp.concatenate([low, block, high], axis=dim)
    return block


def strain_parts(inner, padded):
    grads = []
    for i in range(3):
        field = inner[i]
        beside_all = padded[i]
        along_x = (jnp.roll(field, -1, -1) - jnp.roll(field, 1, -1)) * 0.5
        along_y = (beside_all[1:-1, 2:, :] - beside_all[1:-1, :-2, :]) * 0.5
        along_z = (beside_all[2:, 1:-1, :] - beside_all[:-2, 1:-1, :]) * 0.5
        grads.append([along_x, along_y, along_z])
    strain = [0.5 * (grads[i][j] + grads[j][i]) for i, j in pair_list]
    total = jnp.zeros_like(strain[0])
    for index in range(6):
        total = total + pair_weight[index] * strain[index] * strain[index]
    return (jnp.stack(strain), jnp.sqrt(2.0 * total))


def filter_padded(padded, axis, length):
    result = jnp.zeros_like(lax.slice_in_dim(padded, 0, length, axis=axis))
    for k in range(9):
        result = result + filter_taps[k] * lax.slice_in_dim(padded, k, k + length, axis=axis)
    return result


def filter_along_x(fields):
    result = jnp.zeros_like(fields)
    for k in range(9):
        result = result + filter_taps[k] * jnp.roll(fields, 4 - k, -1)
    return result


def along_y_pencil(piece):
    length = piece.shape[2]
    padded = jnp.pad(piece, ((0, 0), (0, 0), (4, 4), (0, 0)))
    smoothed = filter_padded(padded, 2, length)
    return lax.all_to_all(smoothed, "row", split_axis=2, concat_axis=3, tiled=True)


def build_fields(vel, strain, magnitude):
    products = jnp.stack([vel[i] * vel[j] for i, j in pair_list])
    return jnp.concatenate([vel, products, magnitude[None] * strain], axis=0)


def on_device(velocity):
    depth_y = velocity.shape[2]
    depth_z = velocity.shape[1]
    planes = padded_2(velocity, (("col", 1),), 1)
    reach = 1
    extended = padded_2(planes, (("row", 2),), reach)
    strain, magnitude = strain_parts(velocity, extended)
    fields = build_fields(velocity, strain, magnitude)
    along_x = filter_along_x(fields)
    along_y = along_y_pencil(
        lax.all_to_all(along_x, "row", split_axis=3, concat_axis=2, tiled=True)
    )
    rims_z = padded_2(along_y, (("col", 1),), 4)
    filtered = filter_padded(rims_z, 1, depth_z)
    bar_vel = filtered[0:3]
    leonard = jnp.stack(
        [filtered[3 + index] - bar_vel[i] * bar_vel[j] for index, (i, j) in enumerate(pair_list)]
    )
    bar_faces = padded_2(bar_vel, (("row", 2), ("col", 1)), 1)
    bar_strain, bar_mag = strain_parts(bar_vel, bar_faces)
    model = 2.0 * (filtered[9:15] - 4.0 * bar_mag[None] * bar_strain)
    numer = jnp.zeros((depth_y,), jnp.float32)
    denom = jnp.zeros((depth_y,), jnp.float32)
    for index in range(6):
        numer = numer + jnp.sum(pair_weight[index] * leonard[index] * model[index], axis=(0, 2))
        denom = denom + jnp.sum(pair_weight[index] * model[index] * model[index], axis=(0, 2))
    numer, denom = lax.psum((numer, denom), "col")
    count = velocity.shape[3] * depth_z * lax.axis_size("col")
    coeff = jnp.maximum(numer / count / (denom / count + 1e-06), 0.0)
    stress = -2.0 * coeff[None, None, :, None] * magnitude[None] * strain
    return (leonard, model, stress)


def solution(mesh):
    placed = (P(None, "col", "row", None),)
    return jax.shard_map(
        on_device,
        mesh=mesh,
        in_specs=placed,
        out_specs=(
            P(None, "col", "row", None),
            P(None, "col", "row", None),
            P(None, "col", "row", None),
        ),
        check_vma=False,
    )
```

profile of v0, /device:TPU:25, one launch (start us, length us, event | category | flops | bytes accessed | tf_op | source)
XLA Modules:
  0.0 909.5 jit_solution(16666840177329481572)
XLA Ops:
  1.9 5.5 collective-permute-start
  9.3 2.8 collective-permute-done
  12.2 3.0 constant_dynamic-update-slice_fusion.1
  22.2 3.1 collective-permute-start.2
  25.3 6.8 collective-permute-start.3
  40.5 2.1 multiply_dynamic-update-slice_fusion
  42.6 13.2 %fusion.98 = (f32[15,4,8,4092]{3,2,1,0:T(8,128)}, f32[15,4,8,4092]{3,2,1,0:T(8,128)}) fusion(f32[15,4,8,4096]{3,2,1,0:T(8,128)} %multiply_dynamic-update-slice_fusion), kind=kLoop, calls=%fused_computation.212 | loop fusion | bytes 31426560 | tf_op jit(solution)/shard_map/jit(_roll_static)/slice | solution.py:60
  55.8 13.2 %fusion.100 = (f32[15,4,8,4093]{3,2,1,0:T(8,128)}, f32[15,4,8,4093]{3,2,1,0:T(8,128)}) fusion(f32[15,4,8,4096]{3,2,1,0:T(8,128)} %multiply_dynamic-update-slice_fusion), kind=kLoop, calls=%fused_computation.214 | loop fusion | bytes 31434240 | tf_op jit(solution)/shard_map/jit(_roll_static)/slice | solution.py:60
  69.0 13.2 %fusion.102 = (f32[15,4,8,4094]{3,2,1,0:T(8,128)}, f32[15,4,8,4094]{3,2,1,0:T(8,128)}) fusion(f32[15,4,8,4096]{3,2,1,0:T(8,128)} %multiply_dynamic-update-slice_fusion), kind=kLoop, calls=%fused_computation.216 | loop fusion | bytes 31441920 | tf_op jit(solution)/shard_map/jit(_roll_static)/slice | solution.py:60
  82.2 13.3 %fusion.104 = (f32[15,4,8,4095]{3,2,1,0:T(8,128)}, f32[15,4,8,4095]{3,2,1,0:T(8,128)}) fusion(f32[15,4,8,4096]{3,2,1,0:T(8,128)} %multiply_dynamic-update-slice_fusion), kind=kLoop, calls=%fused_computation.218 | loop fusion | bytes 31449600 | tf_op jit(solution)/shard_map/jit(_roll_static)/slice | solution.py:60
  100.3 28.0 %fusion.25 = f32[15,4,8,4096]{3,2,1,0:T(8,128)} fusion(f32[15,4,8,4092]{3,2,1,0:T(8,128)} %get-tuple-element.38, f32[15,4,8,4]{3,2,1,0:T(8,128)S(1)} %get-tuple-element.40, f32[15,4,8,4093]{3,2,1,0:T(8,128)} %get-tuple-element.42, f32[15,4,8,3]{3,2,1,0:T(8,128)S(1)} %get-tuple-element.44, f32[15,4,8,4094]{3,2,1,0:T(8,128)} %get-tuple-element.46, ...), kind=kLoop, calls=%fused_computation.36 | loop fusion | flops 49152000 | bytes 78643200 | tf_op jit(solution)/shard_map/add | solution.py:60
  128.3 35.1 %copy.194 = f32[15,4,8,4096]{0,2,1,3:T(8,128)} copy(f32[15,4,8,4096]{3,2,1,0:T(8,128)} %fusion.25) | data formatting | bytes 15728640 | tf_op jit(solution)/shard_map/add | solution.py:60
  163.3 58.5 %reshape.137 = f32[32,1,61440]{2,1,0:T(1,128)} reshape(f32[4096,4,8,15]{3,2,1,0:T(8,128)} %bitcast.165) | data formatting | bytes 15728640
  221.9 90.4 %all_to_all.36 = f32[32,1,61440]{2,1,0:T(1,128)} all-to-all(f32[32,1,61440]{2,1,0:T(1,128)} %reshape.137), channel_id=1, replica_groups=mesh['row'=32,'col'=8] {'row'}, dimensions={0} | all-to-all | bytes 15728640 | tf_op jit(solution)/shard_map/all_to_all | solution.py:86
  312.8 24.8 %reduce = f32[32,61440]{1,0:T(8,128)} reduce(f32[32,1,61440]{2,1,0:T(1,128)} %all_to_all.36, f32[]{:T(128)} %broadcast.127), dimensions={1}, to_apply=%all_to_all.26.reduce_sub_computation | reduce | bytes 15728644 | tf_op jit(solution)/shard_map/all_to_all | solution.py:86
  337.6 106.1 %reshape.138 = f32[4096,4,8,15]{3,2,1,0:T(8,128)} reshape(f32[32,61440]{1,0:T(8,128)} %reduce) | data formatting | bytes 15728640
  443.7 47.2 %copy.195 = f32[15,4,32,8,128]{4,1,0,3,2:T(4,128)} copy(f32[15,4,32,8,128]{0,3,1,4,2:T(8,128)} %bitcast.16) | data formatting | bytes 15728640 | tf_op jit(solution)/shard_map/all_to_all | solution.py:86
  490.9 30.0 %multiply_add_fusion = f32[15,4,256,128]{3,1,0,2:T(4,128)S(1)} fusion(f32[15,4,256,128]{3,1,0,2:T(4,128)} %bitcast.168), kind=kLoop, calls=%fused_computation.45 | loop fusion | flops 33423360 | bytes 15728640 | tf_op jit(solution)/shard_map/add | solution.py:53
  520.9 91.5 %all_to_all.37 = f32[15,4,256,128]{3,1,0,2:T(4,128)S(1)} all-to-all(f32[15,4,256,128]{3,1,0,2:T(4,128)S(1)} %multiply_add_fusion), channel_id=1, replica_groups=mesh['row'=32,'col'=8] {'row'}, dimensions={2} | all-to-all | bytes 15728640 | tf_op jit(solution)/shard_map/all_to_all | solution.py:68
  613.5 24.8 %collective-permute-start.4 = (f32[15,4,8,4096]{3,2,1,0:T(8,128)S(1)}, f32[15,4,8,4096]{3,2,1,0:T(8,128)S(1)}, u32[]{:S(2)}, u32[]{:S(2)}) collective-permute-start(f32[15,4,8,4096]{3,2,1,0:T(8,128)S(1)} %bitcast.170), channel_id=1, source_target_pairs={{0,1},{1,2},{2,3},{3,4},{4,5},{5,6},{6,7},{8,9},{9,10},{10,11},{11... | collective-permute-start | bytes 23592968 | tf_op jit(solution)/shard_map/ppermute | solution.py:26
  640.2 85.0 %collective-permute-done.4 = f32[15,4,8,4096]{3,2,1,0:T(8,128)S(1)} collective-permute-done((f32[15,4,8,4096]{3,2,1,0:T(8,128)S(1)}, f32[15,4,8,4096]{3,2,1,0:T(8,128)S(1)}, u32[]{:S(2)}, u32[]{:S(2)}) %collective-permute-start.4) | collective-permute-done | bytes 7864352 | tf_op jit(solution)/shard_map/ppermute | solution.py:26
  725.2 3.1 copy-done.5
  728.3 84.4 %collective-permute-done.5 = f32[15,4,8,4096]{3,2,1,0:T(8,128)} collective-permute-done((f32[15,4,8,4096]{3,2,1,0:T(8,128)S(1)}, f32[15,4,8,4096]{3,2,1,0:T(8,128)}, u32[]{:S(2)}, u32[]{:S(2)}) %collective-permute-start.5) | collective-permute-done | bytes 7864352 | tf_op jit(solution)/shard_map/ppermute | solution.py:29
  812.7 27.3 %fusion.4 = f32[15,4,8,4096]{3,2,1,0:T(8,128)} fusion(f32[15,4,8,4096]{3,2,1,0:T(8,128)} %bitcast.172, f32[15,4,8,4096]{3,2,1,0:T(8,128)} %collective-permute-done.5, f32[15,4,8,4096]{3,2,1,0:T(8,128)} %copy-done.5), kind=kLoop, calls=%fused_computation.12 | loop fusion | flops 45219840 | bytes 31457280 | tf_op jit(solution)/shard_map/add | solution.py:53
  841.7 2.5 fusion.97
  849.1 2.8 collective-permute-start.6
  852.0 5.5 collective-permute-start.7
  860.6 4.6 collective-permute-start.8
  867.5 6.7 collective-permute-done.8
  874.2 13.2 %collective-permute-done.9 = f32[3,1,10,4096]{3,2,1,0:T(8,128)S(1)} collective-permute-done((f32[3,1,10,4096]{3,2,1,0:T(8,128)S(1)}, f32[3,1,10,4096]{3,2,1,0:T(8,128)S(1)}, u32[]{:S(2)}, u32[]{:S(2)}) %collective-permute-start.9) | collective-permute-done | bytes 491552 | tf_op jit(solution)/shard_map/ppermute | solution.py:29
  892.4 11.9 %all-reduce.1 = (f32[8]{0:T(128)S(1)}, f32[8]{0:T(128)S(1)}) all-reduce(f32[8]{0:T(128)S(1)} %add_add_fusion, f32[8]{0:T(128)S(1)} %add_add_fusion.1), channel_id=1, replica_groups=mesh['row'=32,'col'=8] {'col'}, use_global_device_ids=true, to_apply=%region_13.14 | all-reduce | flops 16 | bytes 128 | tf_op jit(solution)/shard_map/psum | solution.py:102
  905.4 3.9 broadcast_multiply_fusion
  (86 shorter events, 44.8 us)
Async XLA Ops:
  0.6 16.4 %copy-start.1 = (f32[3,4,8,4096]{3,2,1,0:T(8,128)S(1)}, f32[3,4,8,4096]{3,2,1,0:T(8,128)}, u32[]{:S(2)}) copy-start(f32[3,4,8,4096]{3,2,1,0:T(8,128)} %param.1) | copy-start | bytes 4718596
  1.9 10.2 %collective-permute-start = (f32[3,1,8,4096]{3,2,1,0:T(8,128)S(1)}, f32[3,1,8,4096]{3,2,1,0:T(8,128)S(1)}, u32[]{:S(2)}, u32[]{:S(2)}) collective-permute-start(f32[3,1,8,4096]{3,2,1,0:T(8,128)S(1)} %get-tuple-element.68), channel_id=1, source_target_pairs={{0,1},{1,2},{2,3},{3,4},{4,5},{5,6},{6,7},{8,9},{9,10},{10,11},{11... | collective-permute-start | bytes 1179656 | tf_op jit(solution)/shard_map/ppermute | solution.py:26
  7.4 14.2 %collective-permute-start.1 = (f32[3,1,8,4096]{3,2,1,0:T(8,128)S(1)}, f32[3,1,8,4096]{3,2,1,0:T(8,128)S(1)}, u32[]{:S(2)}, u32[]{:S(2)}) collective-permute-start(f32[3,1,8,4096]{3,2,1,0:T(8,128)S(1)} %get-tuple-element.67), channel_id=1, source_target_pairs={{1,0},{2,1},{3,2},{4,3},{5,4},{6,5},{7,6},{9,8},{10,9},{11,10},{12... | collective-permute-start | bytes 1179656 | tf_op jit(solution)/shard_map/ppermute | solution.py:29
  22.2 12.3 %collective-permute-start.2 = (f32[3,6,1,4096]{3,2,1,0:T(1,128)S(1)}, f32[3,6,1,4096]{3,2,1,0:T(1,128)S(1)}, u32[]{:S(2)}, u32[]{:S(2)}) collective-permute-start(f32[3,6,1,4096]{3,2,1,0:T(1,128)S(1)} %get-tuple-element.59), channel_id=1, source_target_pairs={{0,8},{8,16},{16,24},{24,32},{32,40},{40,48},{48,56},{56,64},{64,7... | collective-permute-start | bytes 884744 | tf_op jit(solution)/shard_map/ppermute | solution.py:26
  25.3 10.5 %collective-permute-start.3 = (f32[3,6,1,4096]{3,2,1,0:T(1,128)S(1)}, f32[3,6,1,4096]{3,2,1,0:T(1,128)S(1)}, u32[]{:S(2)}, u32[]{:S(2)}) collective-permute-start(f32[3,6,1,4096]{3,2,1,0:T(1,128)S(1)} %get-tuple-element.60), channel_id=1, source_target_pairs={{8,0},{16,8},{24,16},{32,24},{40,32},{48,40},{56,48},{64,56},{72,6... | collective-permute-start | bytes 884744 | tf_op jit(solution)/shard_map/ppermute | solution.py:29
  38.5 0.8 copy-start.6
  38.8 1.7 copy-start.4
  613.5 24.8 %copy-start.2 = (f32[15,4,32,8,128]{4,3,2,1,0:T(8,128)}, f32[15,4,32,8,128]{4,3,2,1,0:T(8,128)S(1)}, u32[]{:S(2)}) copy-start(f32[15,4,32,8,128]{4,3,2,1,0:T(8,128)S(1)} %copy.204) | copy-start | bytes 23592964
  613.5 111.7 %collective-permute-start.4 = (f32[15,4,8,4096]{3,2,1,0:T(8,128)S(1)}, f32[15,4,8,4096]{3,2,1,0:T(8,128)S(1)}, u32[]{:S(2)}, u32[]{:S(2)}) collective-permute-start(f32[15,4,8,4096]{3,2,1,0:T(8,128)S(1)} %bitcast.170), channel_id=1, source_target_pairs={{0,1},{1,2},{2,3},{3,4},{4,5},{5,6},{6,7},{8,9},{9,10},{10,11},{11... | collective-permute-start | bytes 23592968 | tf_op jit(solution)/shard_map/ppermute | solution.py:26
  638.3 174.4 %collective-permute-start.5 = (f32[15,4,8,4096]{3,2,1,0:T(8,128)S(1)}, f32[15,4,8,4096]{3,2,1,0:T(8,128)}, u32[]{:S(2)}, u32[]{:S(2)}) collective-permute-start(f32[15,4,8,4096]{3,2,1,0:T(8,128)S(1)} %bitcast.171), channel_id=1, source_target_pairs={{1,0},{2,1},{3,2},{4,3},{5,4},{6,5},{7,6},{9,8},{10,9},{11,10},{12... | collective-permute-start | bytes 23592968 | tf_op jit(solution)/shard_map/ppermute | solution.py:29
  725.2 3.1 copy-start.5
  840.0 8.3 copy-start
  848.6 12.0 %copy-start.7 = (f32[6,4,8,4096]{3,2,1,0:T(8,128)}, f32[6,4,8,4096]{3,2,1,0:T(8,128)S(1)}, u32[]{:S(2)}) copy-start(f32[6,4,8,4096]{3,2,1,0:T(8,128)S(1)} %get-tuple-element.32) | copy-start | bytes 9437188
  849.1 9.4 %collective-permute-start.6 = (f32[3,4,1,4096]{3,1,2,0:T(4,128)S(1)}, f32[3,4,1,4096]{3,1,2,0:T(4,128)S(1)}, u32[]{:S(2)}, u32[]{:S(2)}) collective-permute-start(f32[3,4,1,4096]{3,1,2,0:T(4,128)S(1)} %copy.197), channel_id=1, source_target_pairs={{0,8},{8,16},{16,24},{24,32},{32,40},{40,48},{48,56},{56,64},{64,7... | collective-permute-start | bytes 589832 | tf_op jit(solution)/shard_map/ppermute | solution.py:26
  852.0 8.1 collective-permute-start.7
  860.6 13.6 %collective-permute-start.8 = (f32[3,1,10,4096]{3,2,1,0:T(8,128)S(1)}, f32[3,1,10,4096]{3,2,1,0:T(8,128)S(1)}, u32[]{:S(2)}, u32[]{:S(2)}) collective-permute-start(f32[3,1,10,4096]{3,2,1,0:T(8,128)S(1)} %get-tuple-element.61), channel_id=1, source_target_pairs={{0,1},{1,2},{2,3},{3,4},{4,5},{5,6},{6,7},{8,9},{9,10},{10,11},{11... | collective-permute-start | bytes 1474568 | tf_op jit(solution)/shard_map/ppermute | solution.py:26
  865.3 22.2 %collective-permute-start.9 = (f32[3,1,10,4096]{3,2,1,0:T(8,128)S(1)}, f32[3,1,10,4096]{3,2,1,0:T(8,128)S(1)}, u32[]{:S(2)}, u32[]{:S(2)}) collective-permute-start(f32[3,1,10,4096]{3,2,1,0:T(8,128)S(1)} %get-tuple-element.62), channel_id=1, source_target_pairs={{1,0},{2,1},{3,2},{4,3},{5,4},{6,5},{7,6},{9,8},{10,9},{11,10},{12... | collective-permute-start | bytes 1474568 | tf_op jit(solution)/shard_map/ppermute | solution.py:29
  890.9 18.4 %copy-start.3 = (f32[6,4,8,4096]{3,2,1,0:T(8,128)}, f32[6,4,8,4096]{3,2,1,0:T(8,128)S(1)}, u32[]{:S(2)}) copy-start(f32[6,4,8,4096]{3,2,1,0:T(8,128)S(1)} %fusion.31) | copy-start | bytes 9437188
where the time goes:
time: 926 us; the launch traced here: 909 us
  local copies, waits for them, and re-layouts  323 us (35%)
  waiting for transfers between devices  197 us (21%)
  blocking collectives  194 us (21%)
  other arithmetic  135 us (15%)
  starting transfers between devices  58.9 us (6%)
    unnamed x20, local copies, waits for them, and re-layouts  172 us
    ppermute x5, waiting for transfers between devices, padded_2(): lax.ppermute(lax.slice_in_dim(block, 0, width, axis=dim), axis, backward)  102 us
    ppermute x5, waiting for transfers between devices, padded_2(): lax.ppermute(lax.slice_in_dim(block, block.shape[dim] - width, None, axis...  95 us
    all_to_all x1, blocking collectives, along_y_pencil(): lax.all_to_all(smoothed, 'row', split_axis=2, concat_axis=3, tiled=True)  91.5 us
    all_to_all x1, blocking collectives, on_device(): lax.all_to_all(along_x, 'row', split_axis=3, concat_axis=2, tiled=True)  90.4 us
    slice x8, local copies, waits for them, and re-layouts, filter_along_x(): result = result + filter_taps[k] * jnp.roll(fields, 4 - k, -1)  57.7 us
    add x2, other arithmetic, filter_padded(): result + filter_taps[k] * lax.slice_in_dim(padded, k, k + length, axis=axis)  57.2 us
    all_to_all x2, local copies, waits for them, and re-layouts, on_device(): lax.all_to_all(along_x, 'row', split_axis=3, concat_axis=2, tiled=True)  47.8 us
  transfers between devices with their start and end apart: 10, of which 9 were waited for; matrix products, arithmetic and copies ran while one was open for 1% of the time, Pallas kernels for 0%

commit v1 on v0

v1 whole, which is shorter than its diff:
```python
import functools

import jax
import jax.numpy as jnp
import numpy as np
from jax import lax
from jax.experimental import pallas as pl
from jax.experimental.pallas import tpu as pltpu
from jax.sharding import PartitionSpec as P

MESH = pl.DeviceIdType.MESH
HBM = pltpu.MemorySpace.HBM
VMEM = pltpu.MemorySpace.VMEM
pair_list = ((0, 0), (0, 1), (0, 2), (1, 1), (1, 2), (2, 2))
pair_weight = (1.0, 2.0, 2.0, 1.0, 2.0, 1.0)

DZ = 4
DY = 8
H = 5
EZ = DZ + 2 * H
EY = DY + 2 * H
VMEM_LIMIT = 60 * 1024 * 1024


def shifted(u, by):
    nt = u.shape[0]
    lane = lax.broadcasted_iota(jnp.int32, u.shape, 1)
    if by == 1:
        near = pltpu.roll(u, 127, 1)
        return jnp.where(lane == 127, pltpu.roll(near, nt - 1, 0), near)
    near = pltpu.roll(u, 1, 1)
    return jnp.where(lane == 0, pltpu.roll(near, 1, 0), near)


def double_box(cells):
    for _ in range(2):
        two = [a + b for a, b in zip(cells, cells[1:])]
        four = [a + b for a, b in zip(two, two[2:])]
        cells = [a + b for a, b in zip(four, cells[4:])]
    return cells


def strain_scaled(grads):
    diag = [grads[i][i] for i in range(3)]
    off = [grads[i][j] + grads[j][i] for i, j in ((0, 1), (0, 2), (1, 2))]
    total = 2.0 * (diag[0] * diag[0] + diag[1] * diag[1] + diag[2] * diag[2])
    total = total + (off[0] * off[0] + off[1] * off[1] + off[2] * off[2])
    quarter = jnp.sqrt(total * (1.0 / 64.0))
    diag = [d + d for d in diag]
    return (diag[0], off[0], off[1], diag[1], off[2], diag[2]), quarter


def halo_kernel(rows, cols, nt, vel, fp, fv, ms, e, t, zp, zv, z_send, z_recv, y_send, y_recv, s_send, s_recv):
    r = lax.axis_index("row")
    c = lax.axis_index("col")
    odd = lax.rem(c, 2)
    out = 2 * odd - 1
    sibling = c - out
    outer1, outer2, inner2 = c + out, c + 2 * out, c - 2 * out
    has_outer = jnp.logical_and(outer1 >= 0, outer1 < cols)
    has_inner2 = jnp.logical_and(inner2 >= 0, inner2 < cols)
    has_up = r > 0
    has_down = r < rows - 1

    barrier = pltpu.get_barrier_semaphore()
    partners = (
        (has_up, r - 1, c),
        (has_down, r + 1, c),
        (c >= 0, r, sibling),
        (has_outer, r, outer1),
        (has_outer, r, outer2),
        (has_inner2, r, inner2),
    )
    count = 0
    for there, row, col in partners:

        @pl.when(there)
        def _(row=row, col=col):
            pl.semaphore_signal(barrier, inc=1, device_id=(row, col), device_id_type=MESH)

        count = count + there.astype(jnp.int32)

    @pl.loop(0, 3 * DZ)
    def _(n):
        i, k = n // DZ, lax.rem(n, DZ)
        for x in range(nt):
            e[i, H + k, pl.ds(H * nt + x, DY, stride=nt), :] = vel[i, k, :, x * 128 : (x + 1) * 128]

    def line(q, start=0, size=nt):
        return pl.ds(pl.multiple_of(q * nt + start, 8), size)

    zero = jnp.zeros((nt, 128), jnp.float32)
    mine = H * odd

    def clear(plane0, planes, row0, count_rows):
        @pl.loop(0, 3 * planes * count_rows)
        def _(n):
            i, rest = n // (planes * count_rows), lax.rem(n, planes * count_rows)
            e[i, plane0 + rest // count_rows, line(row0 + lax.rem(rest, count_rows)), :] = zero

    @pl.when(jnp.logical_not(has_up))
    def _():
        clear(mine, EZ - H, 0, H)

    @pl.when(jnp.logical_not(has_down))
    def _():
        clear(mine, EZ - H, H + DY, H)

    @pl.when(jnp.logical_not(has_outer))
    def _():
        clear(odd * (H + DZ), H, 0, EY)

    pl.semaphore_wait(barrier, count)

    def copy(p_src, p_dst, planes, q_src, q_dst, count_rows, send, recv, row, col):
        return pltpu.make_async_remote_copy(
            src_ref=e.at[:, pl.ds(p_src, planes), pl.ds(q_src * nt, count_rows * nt)],
            dst_ref=e.at[:, pl.ds(p_dst, planes), pl.ds(q_dst * nt, count_rows * nt)],
            send_sem=send,
            recv_sem=recv,
            device_id=(row, col),
            device_id_type=MESH,
        )

    own = H
    outer_plane = [4 - j + odd * (5 + 2 * j) for j in range(H)]

    def z_copy(j):
        if j < 4:
            k = j + odd * (3 - 2 * j)
            dst = 9 + j - odd * (5 + 2 * j)
            return copy(own + k, dst, 1, H, H, DY, z_send.at[j], z_recv.at[j], r, outer1)
        return copy(8 - 3 * odd, 13 * odd, 1, H, H, DY, z_send.at[4], z_recv.at[4], r, inner2)

    def y_copies(n):
        plane, planes = (own, DZ) if n == 0 else (outer_plane[n - 1], 1)
        up = copy(plane, plane, planes, H, H + DY, H, y_send.at[0, n], y_recv.at[0, n], r - 1, c)
        down = copy(plane, plane, planes, DY, 0, H, y_send.at[1, n], y_recv.at[1, n], r + 1, c)
        return up, down

    def s_copy(n):
        dst = 1 + 8 * odd
        if n == 0:
            return copy(own, dst, DZ, H, H, DY, s_send.at[0], s_recv.at[0], r, sibling)
        if n == 1:
            return copy(own, dst, DZ, 0, 0, H, s_send.at[1], s_recv.at[1], r, sibling)
        if n == 2:
            return copy(own, dst, DZ, H + DY, H + DY, H, s_send.at[2], s_recv.at[2], r, sibling)
        return copy(outer_plane[0], 13 * odd, 1, 0, 0, EY, s_send.at[3], s_recv.at[3], r, sibling)

    for j in range(4):

        @pl.when(has_outer)
        def _(j=j):
            z_copy(j).start()

    @pl.when(has_inner2)
    def _():
        z_copy(4).start()

    def y_start(n):
        up, down = y_copies(n)

        @pl.when(has_up)
        def _():
            up.start()

        @pl.when(has_down)
        def _():
            down.start()

    def y_wait_recv(n):
        up, down = y_copies(n)

        @pl.when(has_down)
        def _():
            up.wait_recv()

        @pl.when(has_up)
        def _():
            down.wait_recv()

    def y_wait_send(n):
        up, down = y_copies(n)

        @pl.when(has_up)
        def _():
            up.wait_send()

        @pl.when(has_down)
        def _():
            down.wait_send()

    y_start(0)
    s_copy(0).start()
    for j in range(H):

        @pl.when(has_outer)
        def _(j=j):
            z_copy(j).wait_recv()
            y_start(j + 1)

    y_wait_recv(0)
    s_copy(1).start()
    s_copy(2).start()

    @pl.when(has_outer)
    def _():
        y_wait_recv(1)

    s_copy(3).start()
    for j in range(1, H):

        @pl.when(has_outer)
        def _(j=j):
            y_wait_recv(j + 1)

    for n in range(4):
        s_copy(n).wait_recv()

    y_first = r * DY - 4
    z_first = c * DZ - 4

    @pl.loop(0, EY - 2)
    def _(q):
        in_y = jnp.logical_and(y_first + q >= 0, y_first + q < rows * DY)

        @pl.loop(0, EZ - 2)
        def _(p):
            inside = jnp.logical_and(in_y, jnp.logical_and(z_first + p >= 0, z_first + p < cols * DZ))
            u = [e[i, p + 1, line(q + 1), :] for i in range(3)]
            grads = [
                [
                    shifted(u[i], 1) - shifted(u[i], -1),
                    e[i, p + 1, line(q + 2), :] - e[i, p + 1, line(q), :],
                    e[i, p + 2, line(q + 1), :] - e[i, p, line(q + 1), :],
                ]
                for i in range(3)
            ]
            strain, quarter = strain_scaled(grads)
            quarter = quarter * jnp.where(inside, 1.0, 0.0)
            for n, (i, j) in enumerate(pair_list):
                t[n, p] = u[i] * u[j]
                t[6 + n, p] = quarter * strain[n]

        @pl.when(jnp.logical_and(q >= 4, q < 4 + DY))
        def _():
            for n in range(6):
                for k in range(DZ):
                    ms[n, k, q - 4] = t[6 + n, k + 4]

        @pl.loop(0, 12)
        def _(n):
            for x in range(0, nt, 8):
                cells = [t[n, p, x : x + 8] for p in range(EZ - 2)]
                for k, value in enumerate(double_box(cells)):
                    zp[n, k, q, x : x + 8] = value

    @pl.loop(0, 3 * EY)
    def _(n):
        i, q = n // EY, lax.rem(n, EY)
        for x in range(0, nt, 8):
            cells = [e[i, p, line(q, x, 8), :] for p in range(EZ)]
            for k, value in enumerate(double_box(cells)):
                zv[i, k, q, x : x + 8] = value

    @pl.loop(0, 12 * DZ)
    def _(n):
        f, k = n // DZ, lax.rem(n, DZ)
        for x in range(0, nt, 8):
            cells = [zp[f, k, q, x : x + 8] for q in range(EY - 2)]
            for y, value in enumerate(double_box(cells)):
                fp[f, k, y, x : x + 8] = value

    @pl.loop(0, 3 * (DZ + 2))
    def _(n):
        i, k = n // (DZ + 2), lax.rem(n, DZ + 2)
        for x in range(0, nt, 8):
            cells = [zv[i, k, q, x : x + 8] for q in range(EY)]
            for y, value in enumerate(double_box(cells)):
                fv[i, k, y, x : x + 8] = value

    for j in range(4):

        @pl.when(has_outer)
        def _(j=j):
            z_copy(j).wait_send()

    @pl.when(has_inner2)
    def _():
        z_copy(4).wait_send()

    y_wait_send(0)
    for j in range(H):

        @pl.when(has_outer)
        def _(j=j):
            y_wait_send(j + 1)

    for n in range(4):
        s_copy(n).wait_send()


def halo(velocity, rows, cols):
    nt = velocity.shape[-1] // 128
    f32 = functools.partial(jax.ShapeDtypeStruct, dtype=jnp.float32)
    in_vmem = pl.BlockSpec(memory_space=VMEM)
    dma = pltpu.SemaphoreType.DMA
    scratch = lambda *shape: pltpu.VMEM((*shape, nt, 128), jnp.float32)
    return pl.pallas_call(
        functools.partial(halo_kernel, rows, cols, nt),
        out_shape=(f32((12, DZ, DY, nt, 128)), f32((3, DZ + 2, DY + 2, nt, 128)), f32((6, DZ, DY, nt, 128))),
        in_specs=[in_vmem],
        out_specs=(in_vmem, in_vmem, in_vmem),
        scratch_shapes=[
            pltpu.VMEM((3, EZ, EY * nt, 128), jnp.float32),
            scratch(12, EZ - 2),
            scratch(12, DZ, EY - 2),
            scratch(3, DZ + 2, EY),
            dma((5,)),
            dma((5,)),
            dma((2, 6)),
            dma((2, 6)),
            dma((4,)),
            dma((4,)),
        ],
        compiler_params=pltpu.CompilerParams(collective_id=0, has_side_effects=True, vmem_limit_bytes=VMEM_LIMIT),
        name="halo",
    )(velocity)


def band_matrix():
    taps = np.array([1, 2, 3, 4, 5, 4, 3, 2, 1], np.float32)
    center = np.zeros((128, 128), np.float32)
    edge = np.zeros((128, 128), np.float32)
    for source in range(128):
        for k in range(9):
            target = source + k - 4
            if 0 <= target < 128:
                center[source, target] = taps[k]
            else:
                edge[source, target % 128] = taps[k]
    half = np.concatenate([center, edge], axis=1)
    return np.concatenate([half, half], axis=0)


def x_filter(values, band):
    rows, nt, _ = values.shape
    flat = values.reshape(rows * nt, 128)
    high = flat.astype(jnp.bfloat16)
    low = (flat - high.astype(jnp.float32)).astype(jnp.bfloat16)
    both = jnp.dot(jnp.concatenate([high, low], axis=1), band, preferred_element_type=jnp.float32)
    center = both[:, :128].reshape(rows, nt, 128)
    edge = both[:, 128:].reshape(rows, nt, 128)
    lane = lax.broadcasted_iota(jnp.int32, (rows, nt, 128), 2)
    beside = jnp.where(lane < 64, pltpu.roll(edge, 1, 1), pltpu.roll(edge, nt - 1, 1))
    return (center + beside) * (1.0 / 15625.0)


def finish_kernel(nt, edges, band, fp, fv, leonard, model, sums, bar, filtered, native):
    k = pl.program_id(0)

    @pl.when(k == 0)
    def _():
        sums[...] = jnp.zeros_like(sums)

        @pl.loop(0, 3 * (DZ + 2))
        def _(n):
            i, plane = n // (DZ + 2), lax.rem(n, DZ + 2)
            keep = jnp.where(plane == 0, edges[0], jnp.where(plane == DZ + 1, edges[1], 1.0))
            bar[i, plane] = x_filter(fv[i, plane], band[...]) * keep
            bar[i, plane, 0] = bar[i, plane, 0] * edges[2]
            bar[i, plane, DY + 1] = bar[i, plane, DY + 1] * edges[3]

    @pl.loop(0, 12)
    def _(n):
        filtered[n] = x_filter(fp[n, 0], band[...])

    @pl.loop(0, DY)
    def _(y):
        u = [bar[i, k + 1, y + 1] for i in range(3)]
        grads = [
            [
                shifted(u[i], 1) - shifted(u[i], -1),
                bar[i, k + 1, y + 2] - bar[i, k + 1, y],
                bar[i, k + 2, y + 1] - bar[i, k, y + 1],
            ]
            for i in range(3)
        ]
        strain, quarter = strain_scaled(grads)
        scaled = 8.0 * quarter
        row = pl.ds(pl.multiple_of(y * nt, 8), nt)
        numer = jnp.zeros((nt, 128), jnp.float32)
        denom = jnp.zeros((nt, 128), jnp.float32)
        for n, (i, j) in enumerate(pair_list):
            leonard_p = filtered[n, y] - u[i] * u[j]
            model_p = 2.0 * filtered[6 + n, y] - scaled * strain[n]
            native[n, row, :] = leonard_p
            native[6 + n, row, :] = model_p
            weighted = pair_weight[n] * model_p
            numer = numer + weighted * leonard_p
            denom = denom + weighted * model_p
        sums[0, pl.ds(y, 1), :] += jnp.sum(numer, axis=0, keepdims=True)
        sums[1, pl.ds(y, 1), :] += jnp.sum(denom, axis=0, keepdims=True)

    @pl.loop(0, 6)
    def _(n):
        for x in range(nt):
            leonard[n, 0, :, x * 128 : (x + 1) * 128] = native[n, pl.ds(x, DY, stride=nt), :]
            model[n, 0, :, x * 128 : (x + 1) * 128] = native[6 + n, pl.ds(x, DY, stride=nt), :]


def finish(fp, fv, edges, width):
    nt = width // 128
    f32 = functools.partial(jax.ShapeDtypeStruct, dtype=jnp.float32)
    scratch = lambda *shape: pltpu.VMEM((*shape, 128), jnp.float32)
    return pl.pallas_call(
        functools.partial(finish_kernel, nt),
        grid=(DZ,),
        out_shape=(f32((6, DZ, DY, width)), f32((6, DZ, DY, width)), f32((2, DY, 128))),
        in_specs=[
            pl.BlockSpec(memory_space=pltpu.MemorySpace.SMEM),
            pl.BlockSpec((256, 256), lambda k: (0, 0)),
            pl.BlockSpec((12, 1, DY, nt, 128), lambda k: (0, k, 0, 0, 0)),
            pl.BlockSpec((3, DZ + 2, DY + 2, nt, 128), lambda k: (0, 0, 0, 0, 0)),
        ],
        out_specs=(
            pl.BlockSpec((6, 1, DY, width), lambda k: (0, k, 0, 0)),
            pl.BlockSpec((6, 1, DY, width), lambda k: (0, k, 0, 0)),
            pl.BlockSpec((2, DY, 128), lambda k: (0, 0, 0)),
        ),
        scratch_shapes=[scratch(3, DZ + 2, DY + 2, nt), scratch(12, DY, nt), scratch(12, DY * nt)],
        compiler_params=pltpu.CompilerParams(vmem_limit_bytes=VMEM_LIMIT),
        name="finish",
    )(edges, jnp.asarray(band_matrix(), jnp.bfloat16), fp, fv)


def total_kernel(cols, points, sums, coeff, parts, send, recv):
    r = lax.axis_index("row")
    c = lax.axis_index("col")
    barrier = pltpu.get_barrier_semaphore()
    for step in range(1, cols):
        pl.semaphore_signal(barrier, inc=1, device_id=(r, lax.rem(c + step, cols)), device_id_type=MESH)
    pl.semaphore_wait(barrier, cols - 1)
    copies = [
        pltpu.make_async_remote_copy(
            src_ref=sums,
            dst_ref=parts.at[step - 1],
            send_sem=send.at[step - 1],
            recv_sem=recv.at[step - 1],
            device_id=(r, lax.rem(c + step, cols)),
            device_id_type=MESH,
        )
        for step in range(1, cols)
    ]
    for one in copies:
        one.start()
    added = sums[...]
    for step, one in enumerate(copies):
        one.wait_recv()
        added = added + parts[step]
    numer = jnp.sum(added[0], axis=1, keepdims=True) / points
    denom = jnp.sum(added[1], axis=1, keepdims=True) / points
    ratio = jnp.maximum(numer / (denom + 1e-06), 0.0)
    coeff[...] = jnp.broadcast_to(-2.0 * ratio, coeff.shape)
    for one in copies:
        one.wait_send()


def total(sums, cols, points):
    in_vmem = pl.BlockSpec(memory_space=VMEM)
    dma = pltpu.SemaphoreType.DMA
    return pl.pallas_call(
        functools.partial(total_kernel, cols, points),
        out_shape=jax.ShapeDtypeStruct((DY, 128), jnp.float32),
        in_specs=[in_vmem],
        out_specs=in_vmem,
        scratch_shapes=[pltpu.VMEM((cols - 1, 2, DY, 128), jnp.float32), dma((cols - 1,)), dma((cols - 1,))],
        compiler_params=pltpu.CompilerParams(collective_id=1, has_side_effects=True),
        name="total",
    )(sums)


def scale_kernel(nt, coeff, ms, stress):
    for k in range(DZ):
        for x in range(nt):
            stress[0, k, :, x * 128 : (x + 1) * 128] = ms[0, k, pl.ds(x, DY, stride=nt), :] * coeff[...]


def scale(coeff, ms, width):
    nt = width // 128
    return pl.pallas_call(
        functools.partial(scale_kernel, nt),
        grid=(6,),
        out_shape=jax.ShapeDtypeStruct((6, DZ, DY, width), jnp.float32),
        in_specs=[
            pl.BlockSpec((DY, 128), lambda n: (0, 0)),
            pl.BlockSpec((1, DZ, DY * nt, 128), lambda n: (n, 0, 0, 0)),
        ],
        out_specs=pl.BlockSpec((1, DZ, DY, width), lambda n: (n, 0, 0, 0)),
        compiler_params=pltpu.CompilerParams(vmem_limit_bytes=VMEM_LIMIT),
        name="scale",
    )(coeff, ms.reshape(6, DZ, DY * nt, 128))


def on_device(velocity):
    rows, cols = lax.axis_size("row"), lax.axis_size("col")
    width = velocity.shape[-1]
    fp, fv, ms = halo(velocity, rows, cols)
    r, c = lax.axis_index("row"), lax.axis_index("col")
    edges = jnp.stack([c > 0, c < cols - 1, r > 0, r < rows - 1]).astype(jnp.float32)
    leonard, model, sums = finish(fp, fv, edges, width)
    coeff = total(sums, cols, width * DZ * cols)
    return leonard, model, scale(coeff, ms, width)


def solution(mesh):
    placed = P(None, "col", "row", None)
    return jax.shard_map(on_device, mesh=mesh, in_specs=(placed,), out_specs=(placed, placed, placed), check_vma=False)
```

time: 926 us -> 182 us (0.20); the launches traced: 909 us -> 182 us
  local copies, waits for them, and re-layouts: 323 us -> 0 us
  waiting for transfers between devices: 197 us -> 0 us
  blocking collectives: 194 us -> 0 us
  Pallas kernels: 0 us -> 181 us
  other arithmetic: 135 us -> 0.6 us
  starting transfers between devices: 58.9 us -> 0 us
    ppermute x10 -> x0, waiting for transfers between devices: 197 us -> none  [the longest x5 102 us: padded_2(): lax.ppermute(lax.slice_in_dim(block, 0, width, axis=dim), axis, backward)]
    all_to_all x2 -> x0, blocking collectives: 182 us -> none  [the longest x1 91.5 us: along_y_pencil(): lax.all_to_all(smoothed, 'row', split_axis=2, concat_axis=3, tiled=True)]
    pallas_call x0 -> x4, Pallas kernels: none -> 181 us  [the longest x1 114 us: halo(): pl.pallas_call(functools.partial(halo_kernel, rows, cols, nt), out_shape=...]
    unnamed x20 -> x0, local copies, waits for them, and re-layouts: 172 us -> none
    add x5 -> x0, other arithmetic: 85.2 us -> none  [the longest x2 57.2 us: filter_padded(): result + filter_taps[k] * lax.slice_in_dim(padded, k, k + length, axis=axis)]
    slice x24 -> x0, local copies, waits for them, and re-layouts: 65.5 us -> none  [the longest x8 57.7 us: filter_along_x(): result = result + filter_taps[k] * jnp.roll(fields, 4 - k, -1)]
    ppermute x10 -> x0, starting transfers between devices: 58.9 us -> none  [the longest x5 40.8 us: padded_2(): lax.ppermute(lax.slice_in_dim(block, block.shape[dim] - width, None, axis...]
    all_to_all x3 -> x0, local copies, waits for them, and re-layouts: 48.8 us -> none  [the longest x2 47.8 us: on_device(): lax.all_to_all(along_x, 'row', split_axis=3, concat_axis=2, tiled=True)]
  transfers between devices with their start and end apart: 10 -> 0, of which waited for: 9 -> 0; matrix products, arithmetic and copies ran while one was open for 1% -> 0% of each run, Pallas kernels for 0% -> 0%
where the time goes in v1:
time: 182 us
  Pallas kernels  181 us (99%)
    pallas_call x1, Pallas kernels, halo(): pl.pallas_call(functools.partial(halo_kernel, rows, cols, nt), out_shape=...  114 us
    pallas_call x1, Pallas kernels, total(): pl.pallas_call(functools.partial(total_kernel, cols, points), out_shape=j...  35.6 us
    pallas_call x1, Pallas kernels, finish(): pl.pallas_call(functools.partial(finish_kernel, nt), grid=(DZ,), out_shap...  25.3 us
    pallas_call x1, Pallas kernels, scale(): pl.pallas_call(functools.partial(scale_kernel, nt), grid=(6,), out_shape=...  5.93 us

profile of v1, /device:TPU:25, one launch (start us, length us, event | category | flops | bytes accessed | tf_op | source)
XLA Modules:
  0.0 182.0 jit_solution(10502000029958575951)
XLA Ops:
  0.6 0.6 add_convert_fusion.edges
  1.2 113.9 %halo.1 = (f32[12,4,8,32,128]{4,3,2,1,0:T(8,128)}, f32[3,6,10,32,128]{4,3,2,1,0:T(8,128)}, f32[6,4,8,32,128]{4,3,2,1,0:T(8,128)}) custom-call(f32[3,4,8,4096]{3,2,1,0:T(8,128)} %vel.1), custom_call_target="tpu_custom_call" | custom-call | tf_op jit(solution)/shard_map/halo/pallas_call | solution.py:310
  115.2 25.3 %finish.1 = (f32[6,4,8,4096]{3,2,1,0:T(8,128)}, f32[6,4,8,4096]{3,2,1,0:T(8,128)}, f32[2,8,128]{2,1,0:T(8,128)}) custom-call(f32[4]{0:T(128)} %add_convert_fusion.edges, bf16[256,256]{1,0:T(8,128)(2,1)} %constant.17.clone.band, f32[12,4,8,32,128]{4,3,2,1,0:T(8,128)} %get-tuple-element.9.fp, f32[3,6,10,32,128]{4,3,2,1,0:T(8,128)} %get-tuple-element.10.fv), custom_call_target="tpu_custom_call" | custom-call | tf_op jit(solution)/shard_map/finish/pallas_call | solution.py:417
  140.4 35.6 %total.1.coeff = f32[8,128]{1,0:T(8,128)} custom-call(f32[2,8,128]{2,1,0:T(8,128)} %get-tuple-element.13.sums), custom_call_target="tpu_custom_call" | custom-call | tf_op jit(solution)/shard_map/total/pallas_call | solution.py:473
  176.1 5.9 %scale.1 = f32[6,4,8,4096]{3,2,1,0:T(8,128)} custom-call(f32[8,128]{1,0:T(8,128)} %total.1.coeff, f32[6,4,256,128]{3,2,1,0:T(8,128)} %bitcast.5), custom_call_target="tpu_custom_call" | custom-call | tf_op jit(solution)/shard_map/scale/pallas_call | solution.py:492

commit v2 on v1

--- a/solution.py
+++ b/solution.py
@@ -9,7 +9,6 @@
 from jax.sharding import PartitionSpec as P
 
 MESH = pl.DeviceIdType.MESH
-HBM = pltpu.MemorySpace.HBM
 VMEM = pltpu.MemorySpace.VMEM
 pair_list = ((0, 0), (0, 1), (0, 2), (1, 1), (1, 2), (2, 2))
 pair_weight = (1.0, 2.0, 2.0, 1.0, 2.0, 1.0)
@@ -50,7 +49,9 @@
     return (diag[0], off[0], off[1], diag[1], off[2], diag[2]), quarter
 
 
-def halo_kernel(rows, cols, nt, vel, fp, fv, ms, e, t, zp, zv, z_send, z_recv, y_send, y_recv, s_send, s_recv):
+def halo_kernel(rows, cols, nt, vel, fp_out, fv_out, ms_out, e, t, zp, zv, fp, fv, ms, z_send, z_recv, y_send, y_recv, s_send, s_recv, o_sem):
+    groups = nt // 8
+    cuts = [7] + [17 + 8 * g for g in range(groups - 1)] + [7 + nt]
     r = lax.axis_index("row")
     c = lax.axis_index("col")
     odd = lax.rem(c, 2)
@@ -83,20 +84,18 @@
     @pl.loop(0, 3 * DZ)
     def _(n):
         i, k = n // DZ, lax.rem(n, DZ)
-        for x in range(nt):
-            e[i, H + k, pl.ds(H * nt + x, DY, stride=nt), :] = vel[i, k, :, x * 128 : (x + 1) * 128]
-
-    def line(q, start=0, size=nt):
-        return pl.ds(pl.multiple_of(q * nt + start, 8), size)
-
-    zero = jnp.zeros((nt, 128), jnp.float32)
+        for x in range(0, nt, 8):
+            e[i, H + k, H : H + DY, 8 + x : 16 + x, :] = vel[i, k, :, x * 128 : (x + 8) * 128].reshape(DY, 8, 128)
+        e[i, H + k, H : H + DY, 7:8, :] = vel[i, k, :, (nt - 1) * 128 :].reshape(DY, 1, 128)
+
+    zero = jnp.zeros((nt + 16, 128), jnp.float32)
     mine = H * odd
 
     def clear(plane0, planes, row0, count_rows):
         @pl.loop(0, 3 * planes * count_rows)
         def _(n):
             i, rest = n // (planes * count_rows), lax.rem(n, planes * count_rows)
-            e[i, plane0 + rest // count_rows, line(row0 + lax.rem(rest, count_rows)), :] = zero
+            e[i, plane0 + rest // count_rows, row0 + lax.rem(rest, count_rows)] = zero
 
     @pl.when(jnp.logical_not(has_up))
     def _():
@@ -112,10 +111,11 @@
 
     pl.semaphore_wait(barrier, count)
 
-    def copy(p_src, p_dst, planes, q_src, q_dst, count_rows, send, recv, row, col):
+    def copy(g, p_src, p_dst, planes, q_src, q_dst, count_rows, send, recv, row, col):
+        tiles = pl.ds(cuts[g], cuts[g + 1] - cuts[g])
         return pltpu.make_async_remote_copy(
-            src_ref=e.at[:, pl.ds(p_src, planes), pl.ds(q_src * nt, count_rows * nt)],
-            dst_ref=e.at[:, pl.ds(p_dst, planes), pl.ds(q_dst * nt, count_rows * nt)],
+            src_ref=e.at[:, pl.ds(p_src, planes), pl.ds(q_src, count_rows), tiles],
+            dst_ref=e.at[:, pl.ds(p_dst, planes), pl.ds(q_dst, count_rows), tiles],
             send_sem=send,
             recv_sem=recv,
             device_id=(row, col),
@@ -123,206 +123,193 @@
         )
 
     own = H
-    outer_plane = [4 - j + odd * (5 + 2 * j) for j in range(H)]
-
-    def z_copy(j):
-        if j < 4:
-            k = j + odd * (3 - 2 * j)
-            dst = 9 + j - odd * (5 + 2 * j)
-            return copy(own + k, dst, 1, H, H, DY, z_send.at[j], z_recv.at[j], r, outer1)
-        return copy(8 - 3 * odd, 13 * odd, 1, H, H, DY, z_send.at[4], z_recv.at[4], r, inner2)
-
-    def y_copies(n):
-        plane, planes = (own, DZ) if n == 0 else (outer_plane[n - 1], 1)
-        up = copy(plane, plane, planes, H, H + DY, H, y_send.at[0, n], y_recv.at[0, n], r - 1, c)
-        down = copy(plane, plane, planes, DY, 0, H, y_send.at[1, n], y_recv.at[1, n], r + 1, c)
-        return up, down
-
-    def s_copy(n):
+    far = odd * (H + DZ)
+    near = 4 + 5 * odd
+
+    def z_copies(g):
+        return (
+            (has_outer, copy(g, own, 9 - 8 * odd, DZ, H, H, DY, z_send.at[g, 0], z_recv.at[g, 0], r, outer1), has_outer),
+            (has_inner2, copy(g, 8 - 3 * odd, 13 * odd, 1, H, H, DY, z_send.at[g, 1], z_recv.at[g, 1], r, inner2), has_outer),
+        )
+
+    def y_copies(g, kind):
+        plane, planes = ((own, DZ), (far, H))[kind]
+        on = jnp.logical_or(kind == 0, has_outer)
+        up_there, down_there = jnp.logical_and(has_up, on), jnp.logical_and(has_down, on)
+        up = copy(g, plane, plane, planes, H, H + DY, H, y_send.at[g, 0, kind], y_recv.at[g, 0, kind], r - 1, c)
+        down = copy(g, plane, plane, planes, DY, 0, H, y_send.at[g, 1, kind], y_recv.at[g, 1, kind], r + 1, c)
+        return (up_there, up, down_there), (down_there, down, up_there)
+
+    def s_copies(g):
         dst = 1 + 8 * odd
-        if n == 0:
-            return copy(own, dst, DZ, H, H, DY, s_send.at[0], s_recv.at[0], r, sibling)
-        if n == 1:
-            return copy(own, dst, DZ, 0, 0, H, s_send.at[1], s_recv.at[1], r, sibling)
-        if n == 2:
-            return copy(own, dst, DZ, H + DY, H + DY, H, s_send.at[2], s_recv.at[2], r, sibling)
-        return copy(outer_plane[0], 13 * odd, 1, 0, 0, EY, s_send.at[3], s_recv.at[3], r, sibling)
-
-    for j in range(4):
-
-        @pl.when(has_outer)
-        def _(j=j):
-            z_copy(j).start()
-
-    @pl.when(has_inner2)
-    def _():
-        z_copy(4).start()
-
-    def y_start(n):
-        up, down = y_copies(n)
-
-        @pl.when(has_up)
-        def _():
-            up.start()
-
-        @pl.when(has_down)
-        def _():
-            down.start()
-
-    def y_wait_recv(n):
-        up, down = y_copies(n)
-
-        @pl.when(has_down)
-        def _():
-            up.wait_recv()
-
-        @pl.when(has_up)
-        def _():
-            down.wait_recv()
-
-    def y_wait_send(n):
-        up, down = y_copies(n)
-
-        @pl.when(has_up)
-        def _():
-            up.wait_send()
-
-        @pl.when(has_down)
-        def _():
-            down.wait_send()
-
-    y_start(0)
-    s_copy(0).start()
-    for j in range(H):
-
-        @pl.when(has_outer)
-        def _(j=j):
-            z_copy(j).wait_recv()
-            y_start(j + 1)
-
-    y_wait_recv(0)
-    s_copy(1).start()
-    s_copy(2).start()
-
-    @pl.when(has_outer)
-    def _():
-        y_wait_recv(1)
-
-    s_copy(3).start()
-    for j in range(1, H):
-
-        @pl.when(has_outer)
-        def _(j=j):
-            y_wait_recv(j + 1)
-
-    for n in range(4):
-        s_copy(n).wait_recv()
+        yes = c >= 0
+        plan = ((own, dst, DZ, H, DY), (own, dst, DZ, 0, H), (own, dst, DZ, H + DY, H), (near, 13 * odd, 1, 0, EY))
+        return [
+            (yes, copy(g, src, to, planes, q, q, n, s_send.at[g, m], s_recv.at[g, m], r, sibling), yes)
+            for m, (src, to, planes, q, n) in enumerate(plan)
+        ]
+
+    def start(copies):
+        for sends, one, _ in copies:
+            pl.when(sends)(one.start)
+
+    def wait_recv(copies):
+        for _, one, receives in copies:
+            pl.when(receives)(one.wait_recv)
+
+    def wait_send(copies):
+        for sends, one, _ in copies:
+            pl.when(sends)(one.wait_send)
+
+    def forward(g):
+        wait_recv(z_copies(g))
+        start(y_copies(g, 1))
+
+    def share(g):
+        wait_recv(y_copies(g, 0))
+        wait_recv(y_copies(g, 1))
+        start(s_copies(g)[1:])
+
+    for g in range(groups):
+        start(z_copies(g))
+        start(y_copies(g, 0))
+        start(s_copies(g)[:1])
+
+    for g in range(min(2, groups)):
+        forward(g)
+    share(0)
 
     y_first = r * DY - 4
     z_first = c * DZ - 4
 
-    @pl.loop(0, EY - 2)
-    def _(q):
-        in_y = jnp.logical_and(y_first + q >= 0, y_first + q < rows * DY)
-
-        @pl.loop(0, EZ - 2)
-        def _(p):
-            inside = jnp.logical_and(in_y, jnp.logical_and(z_first + p >= 0, z_first + p < cols * DZ))
-            u = [e[i, p + 1, line(q + 1), :] for i in range(3)]
-            grads = [
-                [
-                    shifted(u[i], 1) - shifted(u[i], -1),
-                    e[i, p + 1, line(q + 2), :] - e[i, p + 1, line(q), :],
-                    e[i, p + 2, line(q + 1), :] - e[i, p, line(q + 1), :],
-                ]
-                for i in range(3)
-            ]
-            strain, quarter = strain_scaled(grads)
-            quarter = quarter * jnp.where(inside, 1.0, 0.0)
+    def results(x):
+        tiles = pl.ds(x, 8)
+        g = x // 8
+        return (
+            pltpu.make_async_copy(fp.at[:, :, :, tiles], fp_out.at[:, :, :, tiles], o_sem.at[g, 0]),
+            pltpu.make_async_copy(fv.at[:, :, :, tiles], fv_out.at[:, :, :, tiles], o_sem.at[g, 1]),
+            pltpu.make_async_copy(ms.at[:, :, pl.ds(4, DY), tiles], ms_out.at[:, :, :, tiles], o_sem.at[g, 2]),
+        )
+
+    lane = lax.broadcasted_iota(jnp.int32, (8, 128), 1)
+
+    def compute(x):
+        at = pl.ds(pl.multiple_of(8 + x, 8), 8)
+        before, after = pl.ds(7 + x, 8), pl.ds(9 + x, 8)
+        to = pl.ds(pl.multiple_of(x, 8), 8)
+
+        @pl.loop(0, EY - 2)
+        def _(q):
+            in_y = jnp.where(jnp.logical_and(y_first + q >= 0, y_first + q < rows * DY), 1.0, 0.0)
+            for p in range(EZ - 2):
+                grads = []
+                for i in range(3):
+                    u = e[i, p + 1, q + 1, at, :]
+                    right = pltpu.roll(jnp.where(lane == 0, e[i, p + 1, q + 1, after, :], u), 127, 1)
+                    left = pltpu.roll(jnp.where(lane == 127, e[i, p + 1, q + 1, before, :], u), 1, 1)
+                    grads.append(
+                        [
+                            right - left,
+                            e[i, p + 1, q + 2, at, :] - e[i, p + 1, q, at, :],
+                            e[i, p + 2, q + 1, at, :] - e[i, p, q + 1, at, :],
+                        ]
+                    )
+                strain, quarter = strain_scaled(grads)
+                in_z = jnp.logical_and(z_first + p >= 0, z_first + p < cols * DZ)
+                quarter = quarter * jnp.where(in_z, in_y, 0.0)
+                for n in range(6):
+                    value = quarter * strain[n]
+                    t[n, p] = value
+                    if 4 <= p < 4 + DZ:
+                        ms[n, p - 4, q, to, :] = value
             for n, (i, j) in enumerate(pair_list):
-                t[n, p] = u[i] * u[j]
-                t[6 + n, p] = quarter * strain[n]
-
-        @pl.when(jnp.logical_and(q >= 4, q < 4 + DY))
-        def _():
-            for n in range(6):
-                for k in range(DZ):
-                    ms[n, k, q - 4] = t[6 + n, k + 4]
+                cells = [e[i, p, q + 1, at, :] * e[j, p, q + 1, at, :] for p in range(1, EZ - 1)]
+                for k, value in enumerate(double_box(cells)):
+                    zp[n, k, q] = value
+                for k, value in enumerate(double_box([t[n, p] for p in range(EZ - 2)])):
+                    zp[6 + n, k, q] = value
+
+        @pl.loop(0, EY)
+        def _(q):
+            for i in range(3):
+                for k, value in enumerate(double_box([e[i, p, q, at, :] for p in range(EZ)])):
+                    zv[i, k, q] = value
 
         @pl.loop(0, 12)
-        def _(n):
-            for x in range(0, nt, 8):
-                cells = [t[n, p, x : x + 8] for p in range(EZ - 2)]
-                for k, value in enumerate(double_box(cells)):
-                    zp[n, k, q, x : x + 8] = value
-
-    @pl.loop(0, 3 * EY)
-    def _(n):
-        i, q = n // EY, lax.rem(n, EY)
-        for x in range(0, nt, 8):
-            cells = [e[i, p, line(q, x, 8), :] for p in range(EZ)]
-            for k, value in enumerate(double_box(cells)):
-                zv[i, k, q, x : x + 8] = value
-
-    @pl.loop(0, 12 * DZ)
-    def _(n):
-        f, k = n // DZ, lax.rem(n, DZ)
-        for x in range(0, nt, 8):
-            cells = [zp[f, k, q, x : x + 8] for q in range(EY - 2)]
-            for y, value in enumerate(double_box(cells)):
-                fp[f, k, y, x : x + 8] = value
-
-    @pl.loop(0, 3 * (DZ + 2))
-    def _(n):
-        i, k = n // (DZ + 2), lax.rem(n, DZ + 2)
-        for x in range(0, nt, 8):
-            cells = [zv[i, k, q, x : x + 8] for q in range(EY)]
-            for y, value in enumerate(double_box(cells)):
-                fv[i, k, y, x : x + 8] = value
-
-    for j in range(4):
-
-        @pl.when(has_outer)
-        def _(j=j):
-            z_copy(j).wait_send()
-
-    @pl.when(has_inner2)
-    def _():
-        z_copy(4).wait_send()
-
-    y_wait_send(0)
-    for j in range(H):
-
-        @pl.when(has_outer)
-        def _(j=j):
-            y_wait_send(j + 1)
-
-    for n in range(4):
-        s_copy(n).wait_send()
+        def _(f):
+            for k in range(DZ):
+                for y, value in enumerate(double_box([zp[f, k, q] for q in range(EY - 2)])):
+                    fp[f, k, y, to, :] = value
+
+        @pl.loop(0, DZ + 2)
+        def _(k):
+            for i in range(3):
+                for y, value in enumerate(double_box([zv[i, k, q] for q in range(EY)])):
+                    fv[i, k, y, to, :] = value
+
+        for one in results(x):
+            one.start()
+
+    @pl.loop(0, groups)
+    def _(g):
+        for step in range(groups):
+
+            @pl.when(g == step)
+            def _(step=step):
+                wait_recv(s_copies(step))
+                if step == groups - 1:
+
+                    @pl.loop(0, 3 * EZ)
+                    def _(n):
+                        i, p = n // EZ, lax.rem(n, EZ)
+                        e[i, p, :, 7 + nt : 9 + nt, :] = e[i, p, :, 7:9, :]
+
+        compute(g * 8)
+        for step in range(groups):
+
+            @pl.when(g == step)
+            def _(step=step):
+                if step + 2 < groups:
+                    forward(step + 2)
+                if step + 1 < groups:
+                    share(step + 1)
+
+    for g in range(groups):
+        for one in results(8 * g):
+            one.wait()
+        wait_send(z_copies(g))
+        wait_send(y_copies(g, 0))
+        wait_send(y_copies(g, 1))
+        wait_send(s_copies(g))
 
 
 def halo(velocity, rows, cols):
     nt = velocity.shape[-1] // 128
+    groups = nt // 8
     f32 = functools.partial(jax.ShapeDtypeStruct, dtype=jnp.float32)
-    in_vmem = pl.BlockSpec(memory_space=VMEM)
+    in_hbm = pl.BlockSpec(memory_space=pl.ANY)
     dma = pltpu.SemaphoreType.DMA
-    scratch = lambda *shape: pltpu.VMEM((*shape, nt, 128), jnp.float32)
+    scratch = lambda *shape: pltpu.VMEM((*shape, 128), jnp.float32)
     return pl.pallas_call(
         functools.partial(halo_kernel, rows, cols, nt),
         out_shape=(f32((12, DZ, DY, nt, 128)), f32((3, DZ + 2, DY + 2, nt, 128)), f32((6, DZ, DY, nt, 128))),
-        in_specs=[in_vmem],
-        out_specs=(in_vmem, in_vmem, in_vmem),
+        in_specs=[pl.BlockSpec(memory_space=VMEM)],
+        out_specs=(in_hbm, in_hbm, in_hbm),
         scratch_shapes=[
-            pltpu.VMEM((3, EZ, EY * nt, 128), jnp.float32),
-            scratch(12, EZ - 2),
-            scratch(12, DZ, EY - 2),
-            scratch(3, DZ + 2, EY),
-            dma((5,)),
-            dma((5,)),
-            dma((2, 6)),
-            dma((2, 6)),
-            dma((4,)),
-            dma((4,)),
+            scratch(3, EZ, EY, nt + 16),
+            scratch(6, EZ - 2, 8),
+            scratch(12, DZ, EY - 2, 8),
+            scratch(3, DZ + 2, EY, 8),
+            scratch(12, DZ, DY, nt),
+            scratch(3, DZ + 2, DY + 2, nt),
+            scratch(6, DZ, EY - 2, nt),
+            dma((groups, 2)),
+            dma((groups, 2)),
+            dma((groups, 2, 2)),
+            dma((groups, 2, 2)),
+            dma((groups, 4)),
+            dma((groups, 4)),
+            dma((groups, 3)),
         ],
         compiler_params=pltpu.CompilerParams(collective_id=0, has_side_effects=True, vmem_limit_bytes=VMEM_LIMIT),
         name="halo",

time: 182 us -> 159 us (0.87)
  Pallas kernels: 181 us -> 158 us
    pallas_call x1, Pallas kernels: 114 us -> 95.4 us  [halo(): pl.pallas_call(functools.partial(halo_kernel, rows, cols, nt), out_shape=...]
    pallas_call x1, Pallas kernels: 35.6 us -> 31.4 us  [total(): pl.pallas_call(functools.partial(total_kernel, cols, points), out_shape=j...]
where the time goes in v2:
time: 159 us
  Pallas kernels  158 us (99%)
    pallas_call x1, Pallas kernels, halo(): pl.pallas_call(functools.partial(halo_kernel, rows, cols, nt), out_shape=...  95.4 us
    pallas_call x1, Pallas kernels, total(): pl.pallas_call(functools.partial(total_kernel, cols, points), out_shape=j...  31.4 us
    pallas_call x1, Pallas kernels, finish(): pl.pallas_call(functools.partial(finish_kernel, nt), grid=(DZ,), out_shap...  25.3 us
    pallas_call x1, Pallas kernels, scale(): pl.pallas_call(functools.partial(scale_kernel, nt), grid=(6,), out_shape=...  5.93 us

profile of v2, /device:TPU:25, one launch (start us, length us, event | category | flops | bytes accessed | tf_op | source)
XLA Modules:
  0.0 159.2 jit_solution(5381762520424204965)
XLA Ops:
  0.6 0.6 add_convert_fusion.edges
  1.2 95.4 %halo.1 = (f32[12,4,8,32,128]{4,3,2,1,0:T(8,128)}, f32[3,6,10,32,128]{4,3,2,1,0:T(8,128)}, f32[6,4,8,32,128]{4,3,2,1,0:T(8,128)}) custom-call(f32[3,4,8,4096]{3,2,1,0:T(8,128)} %vel.1), custom_call_target="tpu_custom_call" | custom-call | tf_op jit(solution)/shard_map/halo/pallas_call | solution.py:293
  96.6 25.3 %finish.1 = (f32[6,4,8,4096]{3,2,1,0:T(8,128)}, f32[6,4,8,4096]{3,2,1,0:T(8,128)}, f32[2,8,128]{2,1,0:T(8,128)}) custom-call(f32[4]{0:T(128)} %add_convert_fusion.edges, bf16[256,256]{1,0:T(8,128)(2,1)} %constant.17.clone.band, f32[12,4,8,32,128]{4,3,2,1,0:T(8,128)} %get-tuple-element.9.fp, f32[3,6,10,32,128]{4,3,2,1,0:T(8,128)} %get-tuple-element.10.fv), custom_call_target="tpu_custom_call" | custom-call | tf_op jit(solution)/shard_map/finish/pallas_call | solution.py:404
  121.9 31.4 %total.1.coeff = f32[8,128]{1,0:T(8,128)} custom-call(f32[2,8,128]{2,1,0:T(8,128)} %get-tuple-element.13.sums), custom_call_target="tpu_custom_call" | custom-call | tf_op jit(solution)/shard_map/total/pallas_call | solution.py:460
  153.3 5.9 %scale.1 = f32[6,4,8,4096]{3,2,1,0:T(8,128)} custom-call(f32[8,128]{1,0:T(8,128)} %total.1.coeff, f32[6,4,256,128]{3,2,1,0:T(8,128)} %bitcast.5), custom_call_target="tpu_custom_call" | custom-call | tf_op jit(solution)/shard_map/scale/pallas_call | solution.py:479

commit v3 on v2

v3 whole, which is shorter than its diff:
```python
import functools

import jax
import jax.numpy as jnp
import numpy as np
from jax import lax
from jax.experimental import pallas as pl
from jax.experimental.pallas import tpu as pltpu
from jax.sharding import PartitionSpec as P

MESH = pl.DeviceIdType.MESH
VMEM = pltpu.MemorySpace.VMEM
pair_list = ((0, 0), (0, 1), (0, 2), (1, 1), (1, 2), (2, 2))
pair_weight = (1.0, 2.0, 2.0, 1.0, 2.0, 1.0)

DZ = 4
DY = 8
H = 5
EZ = DZ + 2 * H
EY = DY + 2 * H
VMEM_LIMIT = 60 * 1024 * 1024
FIRST = (("y0", "z0", "s0", "y1", "s1", "y2", "s2", "y3", "s3"), ("p0", "z1", "p1", "z2", "p2", "z3", "p3", "f0"))
LATER = (("f1", "h0"), ("f2", "h1"), ("f3", "h2"), ("h3",))


def shifted(u, by):
    nt = u.shape[0]
    lane = lax.broadcasted_iota(jnp.int32, u.shape, 1)
    if by == 1:
        near = pltpu.roll(u, 127, 1)
        return jnp.where(lane == 127, pltpu.roll(near, nt - 1, 0), near)
    near = pltpu.roll(u, 1, 1)
    return jnp.where(lane == 0, pltpu.roll(near, 1, 0), near)


def double_box(cells):
    for _ in range(2):
        two = [a + b for a, b in zip(cells, cells[1:])]
        four = [a + b for a, b in zip(two, two[2:])]
        cells = [a + b for a, b in zip(four, cells[4:])]
    return cells


def strain_scaled(grads):
    diag = [grads[i][i] for i in range(3)]
    off = [grads[i][j] + grads[j][i] for i, j in ((0, 1), (0, 2), (1, 2))]
    total = 2.0 * (diag[0] * diag[0] + diag[1] * diag[1] + diag[2] * diag[2])
    total = total + (off[0] * off[0] + off[1] * off[1] + off[2] * off[2])
    quarter = jnp.sqrt(total * (1.0 / 64.0))
    diag = [d + d for d in diag]
    return (diag[0], off[0], off[1], diag[1], off[2], diag[2]), quarter


def halo_kernel(rows, cols, nt, vel, fp_out, fv_out, ms_out, e, t, msr, turn, zp, zv, fp, fv, ms, z_send, z_recv, y_send, y_recv, s_send, s_recv, o_sem):
    groups = nt // 8
    cuts = [7] + [17 + 8 * g for g in range(groups - 1)] + [7 + nt]
    r = lax.axis_index("row")
    c = lax.axis_index("col")
    odd = lax.rem(c, 2)
    out = 2 * odd - 1
    sibling = c - out
    outer1, outer2, inner2 = c + out, c + 2 * out, c - 2 * out
    has_outer = jnp.logical_and(outer1 >= 0, outer1 < cols)
    has_inner2 = jnp.logical_and(inner2 >= 0, inner2 < cols)
    place = lax.rem(r, 4)
    helps = jnp.logical_and(jnp.logical_or(place == 1, place == 2), has_outer)
    helped = jnp.logical_and(jnp.logical_or(place == 0, place == 3), has_outer)
    mate = r + 1 - 2 * lax.rem(r, 2)
    has_up = r > 0
    has_down = r < rows - 1

    barrier = pltpu.get_barrier_semaphore()
    partners = (
        (has_up, r - 1, c),
        (has_down, r + 1, c),
        (c >= 0, r, sibling),
        (has_outer, r, outer1),
        (has_outer, r, outer2),
        (has_inner2, r, inner2),
        (has_outer, mate, outer1),
    )
    count = 0
    for there, row, col in partners:

        @pl.when(there)
        def _(row=row, col=col):
            pl.semaphore_signal(barrier, inc=1, device_id=(row, col), device_id_type=MESH)

        count = count + there.astype(jnp.int32)

    @pl.loop(0, 3 * DZ)
    def _(n):
        i, k = n // DZ, lax.rem(n, DZ)
        for x in range(0, nt, 8):
            e[i, H + k, H : H + DY, 8 + x : 16 + x, :] = vel[i, k, :, x * 128 : (x + 8) * 128].reshape(DY, 8, 128)
        e[i, H + k, H : H + DY, 7:8, :] = vel[i, k, :, (nt - 1) * 128 :].reshape(DY, 1, 128)

    zero = jnp.zeros((nt + 16, 128), jnp.float32)
    mine = H * odd

    def clear(plane0, planes, row0, count_rows):
        @pl.loop(0, 3 * planes * count_rows)
        def _(n):
            i, rest = n // (planes * count_rows), lax.rem(n, planes * count_rows)
            e[i, plane0 + rest // count_rows, row0 + lax.rem(rest, count_rows)] = zero

    @pl.when(jnp.logical_not(has_up))
    def _():
        clear(mine, EZ - H, 0, H)

    @pl.when(jnp.logical_not(has_down))
    def _():
        clear(mine, EZ - H, H + DY, H)

    @pl.when(jnp.logical_not(has_outer))
    def _():
        clear(odd * (H + DZ), H, 0, EY)

    pl.semaphore_wait(barrier, count)

    def copy(g, p_src, p_dst, planes, q_src, q_dst, count_rows, send, recv, row, col):
        tiles = pl.ds(cuts[g], cuts[g + 1] - cuts[g])
        return pltpu.make_async_remote_copy(
            src_ref=e.at[:, pl.ds(p_src, planes), pl.ds(q_src, count_rows), tiles],
            dst_ref=e.at[:, pl.ds(p_dst, planes), pl.ds(q_dst, count_rows), tiles],
            send_sem=send,
            recv_sem=recv,
            device_id=(row, col),
            device_id_type=MESH,
        )

    own = H
    far = odd * (H + DZ)
    near = 4 + 5 * odd

    def z_copies(g):
        single = copy(g, 8 - 3 * odd, 13 * odd, 1, H, H, DY, z_send.at[g, 0], z_recv.at[g, 0], r, inner2)
        whole = copy(g, own, 9 - 8 * odd, DZ, H, H, DY, z_send.at[g, 1], z_recv.at[g, 1], r, outer1)
        row = jnp.where(place == 0, H, H + 5)
        part = copy(g, own, 9 - 8 * odd, DZ, row, row, DY - H, z_send.at[g, 2], z_recv.at[g, 2], r, outer1)
        return (helped, part, helped), (helps, whole, helps), (has_inner2, single, has_outer)

    def proxy_copies(g):
        low = place < 2
        src, dst = jnp.where(low, 0, H + DY), jnp.where(low, DY, H)
        one = copy(g, own, 9 - 8 * odd, DZ, src, dst, H, z_send.at[g, 3], z_recv.at[g, 3], mate, outer1)
        return ((helps, one, helped),)

    def y_copies(g, kind):
        plane, planes = ((own, DZ), (far, H))[kind]
        on = jnp.logical_or(kind == 0, has_outer)
        up_there, down_there = jnp.logical_and(has_up, on), jnp.logical_and(has_down, on)
        up = copy(g, plane, plane, planes, H, H + DY, H, y_send.at[g, 0, kind], y_recv.at[g, 0, kind], r - 1, c)
        down = copy(g, plane, plane, planes, DY, 0, H, y_send.at[g, 1, kind], y_recv.at[g, 1, kind], r + 1, c)
        return (up_there, up, down_there), (down_there, down, up_there)

    def s_copies(g):
        dst = 1 + 8 * odd
        yes = c >= 0
        plan = ((own, dst, DZ, H, DY), (own, dst, DZ, 0, H), (own, dst, DZ, H + DY, H))
        plan = plan + tuple((near, 13 * odd, 1, q, n) for _, _, _, q, n in plan)
        return [
            (yes, copy(g, src, to, planes, q, q, n, s_send.at[g, m], s_recv.at[g, m], r, sibling), yes)
            for m, (src, to, planes, q, n) in enumerate(plan)
        ]

    def start(copies):
        for sends, one, _ in copies:
            pl.when(sends)(one.start)

    def wait_recv(copies):
        for _, one, receives in copies:
            pl.when(receives)(one.wait_recv)

    def wait_send(copies):
        for sends, one, _ in copies:
            pl.when(sends)(one.wait_send)

    def proxy(g):
        wait_recv(y_copies(g, 0))
        start(proxy_copies(g))
        start(s_copies(g)[1:3])

    def forward(g):
        wait_recv(z_copies(g))
        wait_recv(proxy_copies(g))
        start(y_copies(g, 1))
        start(s_copies(g)[3:4])

    def share(g):
        wait_recv(y_copies(g, 1))
        start(s_copies(g)[4:])

    acts = {
        "z": lambda g: start(z_copies(g)),
        "y": lambda g: start(y_copies(g, 0)),
        "s": lambda g: start(s_copies(g)[:1]),
        "p": proxy,
        "f": forward,
        "h": share,
    }

    def run(plan):
        for act in plan:
            if int(act[1]) < groups:
                acts[act[0]](int(act[1]))

    for plan in FIRST:
        run(plan)

    y_first = r * DY - 4
    z_first = c * DZ - 4

    def results(x):
        tiles = pl.ds(x * DY if isinstance(x, int) else pl.multiple_of(x * DY, 64), 8 * DY)
        lanes = pl.ds(x * 128 if isinstance(x, int) else pl.multiple_of(x * 128, 1024), 1024)
        g = x // 8
        return (
            pltpu.make_async_copy(fp.at[:, :, tiles], fp_out.at[:, :, tiles], o_sem.at[g, 0]),
            pltpu.make_async_copy(fv.at[:, :, :, tiles], fv_out.at[:, :, :, tiles], o_sem.at[g, 1]),
            pltpu.make_async_copy(ms.at[:, :, :, lanes], ms_out.at[:, :, :, lanes], o_sem.at[g, 2]),
        )

    lane = lax.broadcasted_iota(jnp.int32, (8, 128), 1)

    def compute(x, rest):
        at = pl.ds(pl.multiple_of(8 + x, 8), 8)
        before, after = pl.ds(7 + x, 8), pl.ds(9 + x, 8)
        to = pl.ds(pl.multiple_of(x, 8), 8)

        @pl.loop(6 * rest, 6 + 10 * rest)
        def _(m):
            q = jnp.where(m < 6, m + 5, jnp.where(m < 11, m - 6, m))
            in_y = jnp.where(jnp.logical_and(y_first + q >= 0, y_first + q < rows * DY), 1.0, 0.0)
            for p in range(EZ - 2):
                grads = []
                for i in range(3):
                    u = e[i, p + 1, q + 1, at, :]
                    right = pltpu.roll(jnp.where(lane == 0, e[i, p + 1, q + 1, after, :], u), 127, 1)
                    left = pltpu.roll(jnp.where(lane == 127, e[i, p + 1, q + 1, before, :], u), 1, 1)
                    grads.append(
                        [
                            right - left,
                            e[i, p + 1, q + 2, at, :] - e[i, p + 1, q, at, :],
                            e[i, p + 2, q + 1, at, :] - e[i, p, q + 1, at, :],
                        ]
                    )
                strain, quarter = strain_scaled(grads)
                in_z = jnp.logical_and(z_first + p >= 0, z_first + p < cols * DZ)
                quarter = quarter * jnp.where(in_z, in_y, 0.0)
                for n in range(6):
                    value = quarter * strain[n]
                    t[n, p] = value
                    if 4 <= p < 4 + DZ:
                        msr[n, p - 4, pl.ds(pl.multiple_of(q * 8, 8), 8), :] = value
            for n, (i, j) in enumerate(pair_list):
                cells = [e[i, p, q + 1, at, :] * e[j, p, q + 1, at, :] for p in range(1, EZ - 1)]
                for k, value in enumerate(double_box(cells)):
                    zp[n, k, q] = value
                for k, value in enumerate(double_box([t[n, p] for p in range(EZ - 2)])):
                    zp[6 + n, k, q] = value

        @pl.loop(DY * rest, DY + 2 * H * rest)
        def _(m):
            q = jnp.where(m < DY, m + H, jnp.where(m < DY + H, m - DY, m))
            for i in range(3):
                for k, value in enumerate(double_box([e[i, p, q, at, :] for p in range(EZ)])):
                    zv[i, k, q] = value

        @pl.when(rest == 1)
        def _():
            @pl.loop(0, 6)
            def _(n):
                for k in range(DZ):
                    for j in range(8):
                        ms[n, k, :, pl.ds(pl.multiple_of((x + j) * 128, 128), 128)] = msr[n, k, pl.ds(4 * 8 + j, DY, stride=8), :]

            def turned(slot, dst, values):
                for y, value in enumerate(values):
                    turn[slot, y * 8 : (y + 1) * 8, :] = value
                for j in range(8):
                    dst[pl.ds(pl.multiple_of((x + j) * DY, DY), DY), :] = turn[slot, pl.ds(j, DY, stride=8), :]

            @pl.loop(0, 12)
            def _(f):
                for k in range(DZ):
                    turned(k, fp.at[f, k], double_box([zp[f, k, q] for q in range(EY - 2)]))

            @pl.loop(0, DZ + 2)
            def _(k):
                for i in range(3):
                    values = double_box([zv[i, k, q] for q in range(EY)])
                    turned(2 * i, fv.at[i, k, 0], values[1 : DY + 1])
                    turned(2 * i + 1, fv.at[i, k, 1], [values[DY + 1]] + [values[0]] * (DY - 1))

            for one in results(x):
                one.start()

    @pl.loop(0, 2 * groups)
    def _(turn_of):
        g, rest = turn_of // 2, lax.rem(turn_of, 2)
        for step in range(groups):

            @pl.when(turn_of == 2 * step)
            def _(step=step):
                wait_recv(s_copies(step)[0:4:3])
                if step == groups - 1:

                    @pl.loop(0, 3 * EZ)
                    def _(n):
                        i, p = n // EZ, lax.rem(n, EZ)
                        e[i, p, :, 7 + nt : 9 + nt, :] = e[i, p, :, 7:9, :]

            @pl.when(turn_of == 2 * step + 1)
            def _(step=step):
                wait_recv(s_copies(step)[1:3])
                wait_recv(s_copies(step)[4:])

        compute(g * 8, rest)
        for step in range(groups):

            @pl.when(turn_of == 2 * step)
            def _(step=step):
                run(LATER[step])

    for g in range(groups):
        for one in results(8 * g):
            one.wait()
        wait_send(z_copies(g))
        wait_send(proxy_copies(g))
        wait_send(y_copies(g, 0))
        wait_send(y_copies(g, 1))
        wait_send(s_copies(g))


def halo(velocity, rows, cols):
    nt = velocity.shape[-1] // 128
    groups = nt // 8
    f32 = functools.partial(jax.ShapeDtypeStruct, dtype=jnp.float32)
    in_hbm = pl.BlockSpec(memory_space=pl.ANY)
    dma = pltpu.SemaphoreType.DMA
    scratch = lambda *shape: pltpu.VMEM((*shape, 128), jnp.float32)
    return pl.pallas_call(
        functools.partial(halo_kernel, rows, cols, nt),
        out_shape=(f32((12, DZ, nt * DY, 128)), f32((3, DZ + 2, 2, nt * DY, 128)), f32((6, DZ, DY, nt * 128))),
        in_specs=[pl.BlockSpec(memory_space=VMEM)],
        out_specs=(in_hbm, in_hbm, in_hbm),
        scratch_shapes=[
            scratch(3, EZ, EY, nt + 16),
            scratch(6, EZ - 2, 8),
            scratch(6, DZ, (EY - 2) * 8),
            scratch(6, 8 * DY),
            scratch(12, DZ, EY - 2, 8),
            scratch(3, DZ + 2, EY, 8),
            scratch(12, DZ, nt * DY),
            scratch(3, DZ + 2, 2, nt * DY),
            pltpu.VMEM((6, DZ, DY, nt * 128), jnp.float32),
            dma((groups, 4)),
            dma((groups, 4)),
            dma((groups, 2, 2)),
            dma((groups, 2, 2)),
            dma((groups, 6)),
            dma((groups, 6)),
            dma((groups, 3)),
        ],
        compiler_params=pltpu.CompilerParams(collective_id=0, has_side_effects=True, vmem_limit_bytes=VMEM_LIMIT),
        name="halo",
    )(velocity)


def band_matrix():
    taps = np.array([1, 2, 3, 4, 5, 4, 3, 2, 1], np.float32)
    center = np.zeros((128, 128), np.float32)
    edge = np.zeros((128, 128), np.float32)
    for source in range(128):
        for k in range(9):
            target = source + k - 4
            if 0 <= target < 128:
                center[source, target] = taps[k]
            else:
                edge[source, target % 128] = taps[k]
    half = np.concatenate([center, edge], axis=1)
    return np.concatenate([half, half], axis=0)


SCALE = 1.0 / 15625.0


def x_filter(flat, band, scale):
    high = flat.astype(jnp.bfloat16)
    low = (flat - high.astype(jnp.float32)).astype(jnp.bfloat16)
    both = jnp.dot(jnp.concatenate([high, low], axis=1), band, preferred_element_type=jnp.float32)
    center, edge = both[:, :128], both[:, 128:]
    lane = lax.broadcasted_iota(jnp.int32, flat.shape, 1)
    from_low = jnp.concatenate([edge[-DY:], edge[:-DY]], axis=0)
    from_high = jnp.concatenate([edge[DY:], edge[:DY]], axis=0)
    return (center + jnp.where(lane < 64, from_low, from_high)) * scale


def finish_kernel(rows, cols, nt, band, fp, fv, leonard, model, sums, bar, filtered):
    s = pl.program_id(0)
    shape = (DY, 128)
    lane = lax.broadcasted_iota(jnp.int32, shape, 1)
    line = lax.broadcasted_iota(jnp.int32, shape, 0)

    @pl.when(s == 0)
    def _():
        sums[...] = jnp.zeros_like(sums)

    r, c = lax.axis_index("row"), lax.axis_index("col")
    outside = jnp.logical_or(jnp.logical_and(s == 0, c == 0), jnp.logical_and(s == DZ + 1, c == cols - 1))
    keep = jnp.where(outside, 0.0, SCALE)
    for i in range(3):
        bar[i, s, 0] = x_filter(fv[i, 0, 0], band[...], keep)

    @pl.when(jnp.logical_and(s >= 1, s <= DZ))
    def _():
        below, above = jnp.where(r < rows - 1, 1.0, 0.0), jnp.where(r > 0, 1.0, 0.0)
        beyond = jnp.where(lax.broadcasted_iota(jnp.int32, (nt, DY, 128), 1) == 0, below, above).reshape(nt * DY, 128)
        for i in range(3):
            bar[i, s, 1] = x_filter(fv[i, 0, 1], band[...], SCALE) * beyond

    @pl.when(s >= 2)
    def _():
        k = s - 1

        for n in range(12):
            filtered[n] = x_filter(fp[n, 0], band[...], SCALE)

        @pl.loop(0, nt, step=8, init_carry=(jnp.zeros(shape, jnp.float32),) * 2)
        def totals(x0, carry):
            numer, denom = carry
            for x in range(8):
                x = x0 + x
                before, after = lax.rem(x + nt - 1, nt), lax.rem(x + 1, nt)
                at = lambda i, plane, x, part=0: bar[i, plane, part, pl.ds(pl.multiple_of(x * DY, DY), DY), :]
                u = [at(i, k, x) for i in range(3)]
                grads = []
                for i in range(3):
                    right = pltpu.roll(jnp.where(lane == 0, at(i, k, after), u[i]), 127, 1)
                    left = pltpu.roll(jnp.where(lane == 127, at(i, k, before), u[i]), 1, 1)
                    rim = at(i, k, x, 1)
                    down = pltpu.roll(jnp.where(line == 0, rim, u[i]), DY - 1, 0)
                    up = pltpu.roll(jnp.where(line == DY - 1, rim, u[i]), 1, 0)
                    grads.append([right - left, down - up, at(i, k + 1, x) - at(i, k - 1, x)])
                strain, quarter = strain_scaled(grads)
                scaled = 8.0 * quarter
                here = pl.ds(pl.multiple_of(x * DY, DY), DY)
                lanes = pl.ds(pl.multiple_of(x * 128, 128), 128)
                for n, (i, j) in enumerate(pair_list):
                    leonard_p = filtered[n, here, :] - u[i] * u[j]
                    model_p = 2.0 * filtered[6 + n, here, :] - scaled * strain[n]
                    leonard[n, 0, :, lanes] = leonard_p
                    model[n, 0, :, lanes] = model_p
                    weighted = model_p if pair_weight[n] == 1.0 else 2.0 * model_p
                    numer = numer + weighted * leonard_p
                    denom = denom + weighted * model_p
            return numer, denom

        sums[0] += totals[0]
        sums[1] += totals[1]


def finish(fp, fv, rows, cols, width):
    nt = width // 128
    f32 = functools.partial(jax.ShapeDtypeStruct, dtype=jnp.float32)
    scratch = lambda *shape: pltpu.VMEM((*shape, 128), jnp.float32)
    plane = lambda s: (0, jnp.maximum(s - 2, 0), 0, 0)
    return pl.pallas_call(
        functools.partial(finish_kernel, rows, cols, nt),
        grid=(DZ + 2,),
        out_shape=(f32((6, DZ, DY, width)), f32((6, DZ, DY, width)), f32((2, DY, 128))),
        in_specs=[
            pl.BlockSpec((256, 256), lambda s: (0, 0)),
            pl.BlockSpec((12, 1, nt * DY, 128), plane),
            pl.BlockSpec((3, 1, 2, nt * DY, 128), lambda s: (0, s, 0, 0, 0)),
        ],
        out_specs=(
            pl.BlockSpec((6, 1, DY, width), plane),
            pl.BlockSpec((6, 1, DY, width), plane),
            pl.BlockSpec((2, DY, 128), lambda s: (0, 0, 0)),
        ),
        scratch_shapes=[scratch(3, DZ + 2, 2, nt * DY), scratch(12, nt * DY)],
        compiler_params=pltpu.CompilerParams(vmem_limit_bytes=VMEM_LIMIT),
        name="finish",
    )(jnp.asarray(band_matrix(), jnp.bfloat16), fp, fv)


def total_kernel(cols, points, sums, coeff, own, parts, own_sem, send, recv):
    r = lax.axis_index("row")
    c = lax.axis_index("col")
    load = pltpu.make_async_copy(sums, own, own_sem)
    load.start()
    barrier = pltpu.get_barrier_semaphore()
    for step in range(1, cols):
        pl.semaphore_signal(barrier, inc=1, device_id=(r, lax.rem(c + step, cols)), device_id_type=MESH)
    pl.semaphore_wait(barrier, cols - 1)
    copies = [
        pltpu.make_async_remote_copy(
            src_ref=sums,
            dst_ref=parts.at[step - 1],
            send_sem=send.at[step - 1],
            recv_sem=recv.at[step - 1],
            device_id=(r, lax.rem(c + step, cols)),
            device_id_type=MESH,
        )
        for step in range(1, cols)
    ]
    for one in copies:
        one.start()
    load.wait()
    added = own[...]
    for step, one in enumerate(copies):
        one.wait_recv()
        added = added + parts[step]
    numer = jnp.sum(added[0], axis=1, keepdims=True) / points
    denom = jnp.sum(added[1], axis=1, keepdims=True) / points
    ratio = jnp.maximum(numer / (denom + 1e-06), 0.0)
    coeff[...] = -2.0 * ratio
    for one in copies:
        one.wait_send()


def total(sums, cols, points):
    in_vmem = pl.BlockSpec(memory_space=VMEM)
    dma = pltpu.SemaphoreType.DMA
    return pl.pallas_call(
        functools.partial(total_kernel, cols, points),
        out_shape=jax.ShapeDtypeStruct((DY, 1), jnp.float32),
        in_specs=[pl.BlockSpec(memory_space=pl.ANY)],
        out_specs=in_vmem,
        scratch_shapes=[pltpu.VMEM((2, DY, 128), jnp.float32), pltpu.VMEM((cols - 1, 2, DY, 128), jnp.float32), dma, dma((cols - 1,)), dma((cols - 1,))],
        compiler_params=pltpu.CompilerParams(collective_id=1, has_side_effects=True),
        name="total",
    )(sums)


def on_device(velocity):
    rows, cols = lax.axis_size("row"), lax.axis_size("col")
    width = velocity.shape[-1]
    fp, fv, ms = halo(velocity, rows, cols)
    leonard, model, sums = finish(fp, fv, rows, cols, width)
    coeff = total(sums, cols, width * DZ * cols)
    return leonard, model, ms * coeff[None, None]


def solution(mesh):
    placed = P(None, "col", "row", None)
    return jax.shard_map(on_device, mesh=mesh, in_specs=(placed,), out_specs=(placed, placed, placed), check_vma=False)
```

time: 159 us -> 121 us (0.76)
  Pallas kernels: 158 us -> 116 us
  other arithmetic: 0.6 us -> 2.86 us
    pallas_call x2 -> x1, Pallas kernels: 31.2 us -> 12 us  [finish(): pl.pallas_call(functools.partial(finish_kernel, rows, cols, nt), grid=(DZ...]
    pallas_call x1, Pallas kernels: 31.4 us -> 13.2 us  [total(): pl.pallas_call(functools.partial(total_kernel, cols, points), out_shape=j...]
    pallas_call x1, Pallas kernels: 95.4 us -> 91.1 us  [halo(): pl.pallas_call(functools.partial(halo_kernel, rows, cols, nt), out_shape=...]
    mul x0 -> x1, other arithmetic: none -> 2.07 us  [on_device(): return (leonard, model, ms * coeff[None, None])]
where the time goes in v3:
time: 121 us; the launch traced here: 120 us
  Pallas kernels  116 us (96%)
  other arithmetic  2.86 us (2%)
    pallas_call x1, Pallas kernels, halo(): pl.pallas_call(functools.partial(halo_kernel, rows, cols, nt), out_shape=...  91.1 us
    pallas_call x1, Pallas kernels, total(): pl.pallas_call(functools.partial(total_kernel, cols, points), out_shape=j...  13.2 us
    pallas_call x1, Pallas kernels, finish(): pl.pallas_call(functools.partial(finish_kernel, rows, cols, nt), grid=(DZ...  12 us

profile of v3, /device:TPU:25, one launch (start us, length us, event | category | flops | bytes accessed | tf_op | source)
XLA Modules:
  0.0 119.8 jit_solution(11160966508567031031)
XLA Ops:
  0.6 91.1 %halo.1 = (f32[12,4,256,128]{3,2,1,0:T(8,128)}, f32[3,6,2,256,128]{4,3,2,1,0:T(8,128)}, f32[6,4,8,4096]{3,2,1,0:T(8,128)}) custom-call(f32[3,4,8,4096]{3,2,1,0:T(8,128)} %vel.1), custom_call_target="tpu_custom_call" | custom-call | tf_op jit(solution)/shard_map/halo/pallas_call | solution.py:343
  91.7 0.0 copy-start
  91.7 12.0 %finish.1 = (f32[6,4,8,4096]{3,2,1,0:T(8,128)}, f32[6,4,8,4096]{3,2,1,0:T(8,128)}, f32[2,8,128]{2,1,0:T(8,128)}) custom-call(bf16[256,256]{1,0:T(8,128)(2,1)} %constant.2.clone.band, f32[12,4,256,128]{3,2,1,0:T(8,128)} %get-tuple-element.9.fp, f32[3,6,2,256,128]{4,3,2,1,0:T(8,128)} %get-tuple-element.10.fv), custom_call_target="tpu_custom_call" | custom-call | tf_op jit(solution)/shard_map/finish/pallas_call | solution.py:469
  103.7 13.2 %total.1 = f32[8,1]{1,0:T(8,128)} custom-call(f32[2,8,128]{2,1,0:T(8,128)} %get-tuple-element.14.sums), custom_call_target="tpu_custom_call" | custom-call | tf_op jit(solution)/shard_map/total/pallas_call | solution.py:527
  116.9 0.8 reduce
  117.7 0.0 copy-done
  117.7 2.1 %broadcast_multiply_fusion = f32[6,4,8,4096]{3,2,1,0:T(8,128)} fusion(f32[6,4,8,4096]{3,2,1,0:T(8,128)S(1)} %copy-done, f32[8]{0:T(128)S(1)} %reduce), kind=kLoop, calls=%fused_computation | loop fusion | flops 786432 | bytes 6291488 | tf_op jit(solution)/shard_map/mul | solution.py:544
Async XLA Ops:
  91.7 26.0 %copy-start = (f32[6,4,8,4096]{3,2,1,0:T(8,128)S(1)}, f32[6,4,8,4096]{3,2,1,0:T(8,128)}, u32[]{:S(2)}) copy-start(f32[6,4,8,4096]{3,2,1,0:T(8,128)} %get-tuple-element.13) | copy-start | bytes 9437188

commit v4 on v3

--- a/solution.py
+++ b/solution.py
@@ -19,7 +19,7 @@
 EZ = DZ + 2 * H
 EY = DY + 2 * H
 VMEM_LIMIT = 60 * 1024 * 1024
-FIRST = (("y0", "z0", "s0", "y1", "s1", "y2", "s2", "y3", "s3"), ("p0", "z1", "p1", "z2", "p2", "z3", "p3", "f0"))
+FIRST = (("y0", "z0", "r2", "y1", "r3", "y2", "y3", "s0", "p0"), ("z1", "s1", "p1", "z2", "s2", "p2", "z3", "s3", "p3", "f0"))
 LATER = (("f1", "h0"), ("f2", "h1"), ("f3", "h2"), ("h3",))
 
 
@@ -51,7 +51,9 @@
     return (diag[0], off[0], off[1], diag[1], off[2], diag[2]), quarter
 
 
-def halo_kernel(rows, cols, nt, vel, fp_out, fv_out, ms_out, e, t, msr, turn, zp, zv, fp, fv, ms, z_send, z_recv, y_send, y_recv, s_send, s_recv, o_sem):
+def halo_kernel(rows, cols, nt, vel_in, fp_out, fv_out, ms_out, vel, e, t, msr, turn, zp, zv, fp, fv, ms, z_send, z_recv, y_send, y_recv, s_send, s_recv, o_sem, v_sem):
+    load = pltpu.make_async_copy(vel_in, vel, v_sem)
+    load.start()
     groups = nt // 8
     cuts = [7] + [17 + 8 * g for g in range(groups - 1)] + [7 + nt]
     r = lax.axis_index("row")
@@ -88,12 +90,21 @@
 
         count = count + there.astype(jnp.int32)
 
-    @pl.loop(0, 3 * DZ)
-    def _(n):
-        i, k = n // DZ, lax.rem(n, DZ)
-        for x in range(0, nt, 8):
-            e[i, H + k, H : H + DY, 8 + x : 16 + x, :] = vel[i, k, :, x * 128 : (x + 8) * 128].reshape(DY, 8, 128)
-        e[i, H + k, H : H + DY, 7:8, :] = vel[i, k, :, (nt - 1) * 128 :].reshape(DY, 1, 128)
+    def relay(g):
+        @pl.loop(0, 3)
+        def _(i):
+            for k in range(DZ):
+                own_rows = vel[i, k, :, g * 1024 : (g + 1) * 1024].reshape(DY, 8, 128)
+                e[i, H + k, H : H + DY, 8 + 8 * g : 16 + 8 * g, :] = own_rows
+
+    load.wait()
+    for g in range(min(2, groups)):
+        relay(g)
+
+    @pl.loop(0, 3)
+    def _(i):
+        for k in range(DZ):
+            e[i, H + k, H : H + DY, 7:8, :] = vel[i, k, :, (nt - 1) * 128 :].reshape(DY, 1, 128)
 
     zero = jnp.zeros((nt + 16, 128), jnp.float32)
     mine = H * odd
@@ -192,6 +203,7 @@
         start(s_copies(g)[4:])
 
     acts = {
+        "r": relay,
         "z": lambda g: start(z_copies(g)),
         "y": lambda g: start(y_copies(g, 0)),
         "s": lambda g: start(s_copies(g)[:1]),
@@ -343,9 +355,10 @@
     return pl.pallas_call(
         functools.partial(halo_kernel, rows, cols, nt),
         out_shape=(f32((12, DZ, nt * DY, 128)), f32((3, DZ + 2, 2, nt * DY, 128)), f32((6, DZ, DY, nt * 128))),
-        in_specs=[pl.BlockSpec(memory_space=VMEM)],
+        in_specs=[in_hbm],
         out_specs=(in_hbm, in_hbm, in_hbm),
         scratch_shapes=[
+            pltpu.VMEM(velocity.shape, jnp.float32),
             scratch(3, EZ, EY, nt + 16),
             scratch(6, EZ - 2, 8),
             scratch(6, DZ, (EY - 2) * 8),
@@ -362,6 +375,7 @@
             dma((groups, 6)),
             dma((groups, 6)),
             dma((groups, 3)),
+            dma,
         ],
         compiler_params=pltpu.CompilerParams(collective_id=0, has_side_effects=True, vmem_limit_bytes=VMEM_LIMIT),
         name="halo",
@@ -427,10 +441,10 @@
         for n in range(12):
             filtered[n] = x_filter(fp[n, 0], band[...], SCALE)
 
-        @pl.loop(0, nt, step=8, init_carry=(jnp.zeros(shape, jnp.float32),) * 2)
+        @pl.loop(0, nt, step=32, init_carry=(jnp.zeros(shape, jnp.float32),) * 2)
         def totals(x0, carry):
             numer, denom = carry
-            for x in range(8):
+            for x in range(32):
                 x = x0 + x
                 before, after = lax.rem(x + nt - 1, nt), lax.rem(x + 1, nt)
                 at = lambda i, plane, x, part=0: bar[i, plane, part, pl.ds(pl.multiple_of(x * DY, DY), DY), :]
@@ -516,17 +530,17 @@
     numer = jnp.sum(added[0], axis=1, keepdims=True) / points
     denom = jnp.sum(added[1], axis=1, keepdims=True) / points
     ratio = jnp.maximum(numer / (denom + 1e-06), 0.0)
-    coeff[...] = -2.0 * ratio
+    coeff[...] = jnp.broadcast_to(-2.0 * ratio, coeff.shape)
     for one in copies:
         one.wait_send()
 
 
-def total(sums, cols, points):
+def total(sums, cols, width):
     in_vmem = pl.BlockSpec(memory_space=VMEM)
     dma = pltpu.SemaphoreType.DMA
     return pl.pallas_call(
-        functools.partial(total_kernel, cols, points),
-        out_shape=jax.ShapeDtypeStruct((DY, 1), jnp.float32),
+        functools.partial(total_kernel, cols, width * DZ * cols),
+        out_shape=jax.ShapeDtypeStruct((DY, width), jnp.float32),
         in_specs=[pl.BlockSpec(memory_space=pl.ANY)],
         out_specs=in_vmem,
         scratch_shapes=[pltpu.VMEM((2, DY, 128), jnp.float32), pltpu.VMEM((cols - 1, 2, DY, 128), jnp.float32), dma, dma((cols - 1,)), dma((cols - 1,))],
@@ -540,7 +554,7 @@
     width = velocity.shape[-1]
     fp, fv, ms = halo(velocity, rows, cols)
     leonard, model, sums = finish(fp, fv, rows, cols, width)
-    coeff = total(sums, cols, width * DZ * cols)
+    coeff = total(sums, cols, width)
     return leonard, model, ms * coeff[None, None]
 
 

time: 121 us -> 119 us (0.983)
    pallas_call x1, Pallas kernels: 91.1 us -> 88.8 us  [halo(): pl.pallas_call(functools.partial(halo_kernel, rows, cols, nt), out_shape=...]
    pallas_call x1, Pallas kernels: 13.2 us -> 14.4 us  [total(): pl.pallas_call(functools.partial(total_kernel, cols, width * DZ * cols),...]
where the time goes in v4:
time: 119 us; the launch traced here: 118 us
  Pallas kernels  115 us (97%)
  other arithmetic  2.79 us (2%)
    pallas_call x1, Pallas kernels, halo(): pl.pallas_call(functools.partial(halo_kernel, rows, cols, nt), out_shape=...  88.8 us
    pallas_call x1, Pallas kernels, total(): pl.pallas_call(functools.partial(total_kernel, cols, width * DZ * cols),...  14.4 us
    pallas_call x1, Pallas kernels, finish(): pl.pallas_call(functools.partial(finish_kernel, rows, cols, nt), grid=(DZ...  11.4 us
    mul x1, other arithmetic, on_device(): return (leonard, model, ms * coeff[None, None])  2.79 us

profile of v4, /device:TPU:25, one launch (start us, length us, event | category | flops | bytes accessed | tf_op | source)
XLA Modules:
  0.0 118.1 jit_solution(9459945096303312273)
XLA Ops:
  0.6 88.8 %halo.1 = (f32[12,4,256,128]{3,2,1,0:T(8,128)}, f32[3,6,2,256,128]{4,3,2,1,0:T(8,128)}, f32[6,4,8,4096]{3,2,1,0:T(8,128)}) custom-call(f32[3,4,8,4096]{3,2,1,0:T(8,128)} %vel_in.1), custom_call_target="tpu_custom_call" | custom-call | tf_op jit(solution)/shard_map/halo/pallas_call | solution.py:355
  89.5 0.0 copy-start
  89.5 11.4 %finish.1 = (f32[6,4,8,4096]{3,2,1,0:T(8,128)}, f32[6,4,8,4096]{3,2,1,0:T(8,128)}, f32[2,8,128]{2,1,0:T(8,128)}) custom-call(bf16[256,256]{1,0:T(8,128)(2,1)} %constant.2.clone.band, f32[12,4,256,128]{3,2,1,0:T(8,128)} %get-tuple-element.9.fp, f32[3,6,2,256,128]{4,3,2,1,0:T(8,128)} %get-tuple-element.10.fv), custom_call_target="tpu_custom_call" | custom-call | tf_op jit(solution)/shard_map/finish/pallas_call | solution.py:483
  100.8 14.4 %total.1 = f32[8,4096]{1,0:T(8,128)} custom-call(f32[2,8,128]{2,1,0:T(8,128)} %get-tuple-element.14.sums), custom_call_target="tpu_custom_call" | custom-call | tf_op jit(solution)/shard_map/total/pallas_call | solution.py:541
  115.3 0.0 copy-done
  115.3 2.8 %broadcast_multiply_fusion = f32[6,4,8,4096]{3,2,1,0:T(8,128)} fusion(f32[6,4,8,4096]{3,2,1,0:T(8,128)S(1)} %copy-done, f32[8,4096]{1,0:T(8,128)} %total.1), kind=kLoop, calls=%fused_computation | loop fusion | flops 786432 | bytes 6422528 | tf_op jit(solution)/shard_map/mul | solution.py:558
Async XLA Ops:
  89.5 25.8 %copy-start = (f32[6,4,8,4096]{3,2,1,0:T(8,128)S(1)}, f32[6,4,8,4096]{3,2,1,0:T(8,128)}, u32[]{:S(2)}) copy-start(f32[6,4,8,4096]{3,2,1,0:T(8,128)} %get-tuple-element.13) | copy-start | bytes 9437188

commit v5 on v4

--- a/solution.py
+++ b/solution.py
@@ -19,8 +19,8 @@
 EZ = DZ + 2 * H
 EY = DY + 2 * H
 VMEM_LIMIT = 60 * 1024 * 1024
-FIRST = (("y0", "z0", "r2", "y1", "r3", "y2", "y3", "s0", "p0"), ("z1", "s1", "p1", "z2", "s2", "p2", "z3", "s3", "p3", "f0"))
-LATER = (("f1", "h0"), ("f2", "h1"), ("f3", "h2"), ("h3",))
+FIRST = (("y0", "z0", "r2", "y1", "r3", "y2", "y3", "s0", "p0", "z1"), ("s1", "p1", "z2", "s2", "p2", "z3", "s3", "p3", "f0", "f1"))
+LATER = (("h0",), ("f2", "h1"), ("f3", "h2"), ("h3",))
 
 
 def shifted(u, by):

time: 119 us -> 118 us (level)
    pallas_call x1, Pallas kernels: 14.4 us -> 12.7 us  [total(): pl.pallas_call(functools.partial(total_kernel, cols, width * DZ * cols),...]
    pallas_call x1, Pallas kernels: 88.8 us -> 90.3 us  [halo(): pl.pallas_call(functools.partial(halo_kernel, rows, cols, nt), out_shape=...]
where the time goes in v5:
time: 118 us
  Pallas kernels  114 us (97%)
  other arithmetic  2.79 us (2%)
    pallas_call x1, Pallas kernels, halo(): pl.pallas_call(functools.partial(halo_kernel, rows, cols, nt), out_shape=...  90.3 us
    pallas_call x1, Pallas kernels, total(): pl.pallas_call(functools.partial(total_kernel, cols, width * DZ * cols),...  12.7 us
    pallas_call x1, Pallas kernels, finish(): pl.pallas_call(functools.partial(finish_kernel, rows, cols, nt), grid=(DZ...  11.4 us
    mul x1, other arithmetic, on_device(): return (leonard, model, ms * coeff[None, None])  2.79 us

profile of v5, /device:TPU:25, one launch (start us, length us, event | category | flops | bytes accessed | tf_op | source)
XLA Modules:
  0.0 117.8 jit_solution(16673567178622579697)
XLA Ops:
  0.6 90.3 %halo.1 = (f32[12,4,256,128]{3,2,1,0:T(8,128)}, f32[3,6,2,256,128]{4,3,2,1,0:T(8,128)}, f32[6,4,8,4096]{3,2,1,0:T(8,128)}) custom-call(f32[3,4,8,4096]{3,2,1,0:T(8,128)} %vel_in.1), custom_call_target="tpu_custom_call" | custom-call | tf_op jit(solution)/shard_map/halo/pallas_call | solution.py:355
  90.9 0.0 copy-start
  90.9 11.4 %finish.1 = (f32[6,4,8,4096]{3,2,1,0:T(8,128)}, f32[6,4,8,4096]{3,2,1,0:T(8,128)}, f32[2,8,128]{2,1,0:T(8,128)}) custom-call(bf16[256,256]{1,0:T(8,128)(2,1)} %constant.2.clone.band, f32[12,4,256,128]{3,2,1,0:T(8,128)} %get-tuple-element.9.fp, f32[3,6,2,256,128]{4,3,2,1,0:T(8,128)} %get-tuple-element.10.fv), custom_call_target="tpu_custom_call" | custom-call | tf_op jit(solution)/shard_map/finish/pallas_call | solution.py:483
  102.3 12.7 %total.1 = f32[8,4096]{1,0:T(8,128)} custom-call(f32[2,8,128]{2,1,0:T(8,128)} %get-tuple-element.14.sums), custom_call_target="tpu_custom_call" | custom-call | tf_op jit(solution)/shard_map/total/pallas_call | solution.py:541
  115.0 0.0 copy-done
  115.0 2.8 %broadcast_multiply_fusion = f32[6,4,8,4096]{3,2,1,0:T(8,128)} fusion(f32[6,4,8,4096]{3,2,1,0:T(8,128)S(1)} %copy-done, f32[8,4096]{1,0:T(8,128)} %total.1), kind=kLoop, calls=%fused_computation | loop fusion | flops 786432 | bytes 6422528 | tf_op jit(solution)/shard_map/mul | solution.py:558
Async XLA Ops:
  90.9 24.1 %copy-start = (f32[6,4,8,4096]{3,2,1,0:T(8,128)S(1)}, f32[6,4,8,4096]{3,2,1,0:T(8,128)}, u32[]{:S(2)}) copy-start(f32[6,4,8,4096]{3,2,1,0:T(8,128)} %get-tuple-element.13) | copy-start | bytes 9437188
